TPU v7x, 256 devices: a whole 4x4x8 slice. The times are simulated.
256 devices in a mesh: kv: 8 (over x, y_hi), ctx: 32 (over z, y_lo, core).
Axes of the slice: x: 4, y: 4 (y_hi: 2, y_lo: 2; y = y_hi * 2 + y_lo), z: 8, core: 2. Of those that a mesh axis runs over, the one named last changes fastest.
Arguments:
- queries: bfloat16 [2, 64, 16384], P(None, 'kv'), may hold values from -105 to 105
- kv_cache: bfloat16 [8, 4, 131072, 256], P('kv', None, 'ctx'), may hold values from -5 to 5
- lengths: int32 [64], replicated, may hold values from 16384 to 131071, as said below
Outputs:
- attended: bfloat16 [2, 64, 16384], P(None, 'ctx', 'kv')
Inputs may be any that keep to these rules, and one draw needn't show every extreme that they name: Row r reads lengths[r] + t positions at step t; some row reads exactly 16384 and some row reaches the most.
All inputs are finite; a program needn't handle non-finite values.
Results may differ from a plain program's by a relative error of at most 0.0048.
Values may be sent and summed in bfloat16 or wider, within the bound.
A program may use at most 192 MiB of HBM per device.

v0:
```python
import jax
import jax.numpy as jnp
from jax import lax
from jax.sharding import PartitionSpec as P

MASK_FILLER = -1e30


def from_behind(value, axis, steps):
    count = lax.axis_size(axis)
    pairs = [(source, (source + steps) % count) for source in range(count)]
    return lax.ppermute(value, axis, pairs)


def shard_terms(rollout_queries, cached_keys, cached_values, limits, offset, span_width):
    scores = jnp.einsum(
        "srkgd,kscd->srkgc", rollout_queries, cached_keys, preferred_element_type=jnp.float32
    ) * rollout_queries.shape[-1] ** (-0.5)
    positions = offset + jnp.arange(span_width, dtype=jnp.int32)
    visible = positions[None, None, None, None, :] < limits[:, :, None, None, None]
    masked = jnp.where(visible, scores, MASK_FILLER)
    row_max = jnp.max(masked, axis=-1)
    weights = jnp.where(visible, jnp.exp(masked - row_max[..., None]), 0.0)
    row_sum = jnp.sum(weights, axis=-1)
    weighted = jnp.einsum(
        "srkgc,kscd->srkgd",
        weights.astype(jnp.bfloat16),
        cached_values,
        preferred_element_type=jnp.float32,
    )
    return (row_max, row_sum, weighted)


def combine(first, second):
    highest = jnp.maximum(first[0], second[0])
    first_factor = jnp.exp(first[0] - highest)
    second_factor = jnp.exp(second[0] - highest)
    total = first[1] * first_factor + second[1] * second_factor
    weighted = first[2] * first_factor[..., None] + second[2] * second_factor[..., None]
    return (highest, total, weighted)


def shards(queries, kv_cache, lengths):
    regrouped = lax.all_to_all(queries, "kv", split_axis=2, concat_axis=1, tiled=True)
    step_count, row_count, feature_count = regrouped.shape
    local_heads, seq_count, span_width, double_dim = kv_cache.shape
    head_dim = double_dim // 2
    queries_per_group = feature_count // (local_heads * head_dim)
    member_count = lax.axis_size("ctx")
    member = lax.axis_index("ctx")
    offset = member * span_width
    block_rows = row_count // member_count
    split_cache = kv_cache.reshape(local_heads, seq_count, span_width, 2, head_dim)
    cached_keys = split_cache[:, :, :, 0, :]
    cached_values = split_cache[:, :, :, 1, :]
    partial_list = []
    for decode_step_index in range(step_count):
        rollout_queries = regrouped[decode_step_index].reshape(
            seq_count, row_count // seq_count, local_heads, queries_per_group, head_dim
        )
        limits = (lengths + decode_step_index).reshape(seq_count, row_count // seq_count)
        partial_list.append(
            shard_terms(rollout_queries, cached_keys, cached_values, limits, offset, span_width)
        )
    stacked_max = jnp.stack([entry[0] for entry in partial_list])
    stacked_sum = jnp.stack([entry[1] for entry in partial_list])
    stacked_out = jnp.stack([entry[2] for entry in partial_list])
    flat_max = stacked_max.reshape(step_count, row_count, local_heads, queries_per_group)
    flat_sum = stacked_sum.reshape(step_count, row_count, local_heads, queries_per_group)
    flat_out = stacked_out.reshape(step_count, row_count, local_heads, queries_per_group, head_dim)
    starting_state = (
        jnp.full(
            (step_count, block_rows, local_heads, queries_per_group), MASK_FILLER, jnp.float32
        ),
        jnp.zeros((step_count, block_rows, local_heads, queries_per_group), jnp.float32),
        jnp.zeros((step_count, block_rows, local_heads, queries_per_group, head_dim), jnp.float32),
    )

    def cycle_turn(turn_index, carried_state):
        anchor = (member - turn_index) % member_count
        first_row = anchor * block_rows
        local_part = (
            lax.dynamic_slice_in_dim(flat_max, first_row, block_rows, 1),
            lax.dynamic_slice_in_dim(flat_sum, first_row, block_rows, 1),
            lax.dynamic_slice_in_dim(flat_out, first_row, block_rows, 1),
        )
        updated = combine(carried_state, local_part)
        moved = from_behind((updated[0], updated[1], updated[2]), "ctx", 1)
        return (moved[0], moved[1], moved[2])

    final_state = lax.fori_loop(0, member_count, cycle_turn, starting_state)
    result = final_state[2] / final_state[1][..., None]
    return result.reshape(step_count, block_rows, feature_count).astype(jnp.bfloat16)


def solution(mesh):
    in_specs = (P(None, "kv", None), P("kv", None, "ctx", None), P())
    out_specs = P(None, "ctx", "kv")
    return jax.shard_map(shards, mesh=mesh, in_specs=in_specs, out_specs=out_specs, check_vma=False)
```

profile of v0, /device:TPU:12, one launch (start us, length us, event | category | flops | bytes accessed | tf_op | source)
XLA Modules:
  0.0 305.6 jit_solution(11804124275177603601)
XLA Ops:
  0.0 15.6 %copy.24 = bf16[2,8,16384]{1,0,2:T(2,128)(2,1)} copy(bf16[2,8,16384]{2,1,0:T(8,128)(2,1)} %param.5) | data formatting | bytes 1048576 | tf_op args[0]
  15.6 11.2 %reshape.122 = bf16[8,2,16384]{2,1,0:T(2,128)(2,1)} reshape(bf16[16384,2,8]{2,1,0:T(2,128)(2,1)} %bitcast.123) | data formatting | bytes 1048576
  26.7 6.5 %all-to-all-start = ((bf16[8,2,16384]{2,1,0:T(2,128)(2,1)}), bf16[8,2,16384]{2,1,0:T(2,128)(2,1)S(1)}, u32[]{:S(2)}, u32[]{:S(2)}) async-start(bf16[8,2,16384]{2,1,0:T(2,128)(2,1)} %reshape.122), calls=%async_computation | async-start | bytes 1048576 | tf_op jit(solution)/shard_map/all_to_all | solution.py:44
  33.4 11.5 %copy.22 = bf16[1,4,4096,256]{2,3,1,0:T(8,128)(2,1)} copy(bf16[1,4,4096,256]{3,2,1,0:T(8,128)(2,1)} %param.6) | data formatting | bytes 16777216 | tf_op args[1]
  45.3 10.9 %reshape.123 = bf16[16384,2,8]{2,1,0:T(2,128)(2,1)} reshape(bf16[8,2,16384]{2,1,0:T(2,128)(2,1)S(1)} %all-to-all-done) | data formatting | bytes 1048576
  56.2 17.7 %copy.25 = bf16[2,8,8,2048]{3,1,2,0:T(8,128)(2,1)S(1)} copy(bf16[2,8,8,2048]{1,0,3,2:T(2,128)(2,1)} %bitcast.122) | data formatting | bytes 1048576 | tf_op jit(solution)/shard_map/all_to_all | solution.py:44
  74.0 6.2 %fusion.3 = (f32[4,16,16]{2,1,0:T(8,128)}, f32[4,4096,16,16]{1,3,2,0:T(8,128)S(1)}) fusion(pred[4,16,4096]{2,1,0:T(8,128)(4,1)S(1)} %get-tuple-element.246, bf16[1,4,4096,2,128]{2,4,3,1,0:T(8,128)(2,1)} %bitcast.124, bf16[4,16,16,128]{3,2,1,0:T(8,128)(2,1)S(1)} %bitcast.132), kind=kOutput, calls=%fused_computation.12 | convolution fusion | flops 1086323712 | bytes 21499904 | tf_op jit(solution)/shard_map/srkgd,kscd->srkgc/dot_general | solution.py:16
  80.2 9.8 %fusion.2 = (f32[4,16,16]{2,1,0:T(8,128)}, f32[4,4096,16,16]{1,3,2,0:T(8,128)}) fusion(pred[4,16,4096]{2,1,0:T(8,128)(4,1)S(1)} %get-tuple-element.245, bf16[1,4,4096,2,128]{2,4,3,1,0:T(8,128)(2,1)} %bitcast.125, bf16[4,16,16,128]{3,2,1,0:T(8,128)(2,1)S(1)} %bitcast.131), kind=kOutput, calls=%fused_computation.11 | convolution fusion | flops 1086323712 | bytes 21499904 | tf_op jit(solution)/shard_map/srkgd,kscd->srkgc/dot_general | solution.py:16
  90.0 9.3 %fusion.10 = f32[4,16,16,128]{3,2,1,0:T(8,128)S(1)} fusion(f32[4,4096,16,16]{1,3,2,0:T(8,128)} %get-tuple-element.250, f32[4,16,16]{2,1,0:T(8,128)} %get-tuple-element.249, pred[4,16,4096]{2,1,0:T(8,128)(4,1)S(1)} %get-tuple-element.245, bf16[1,4,4096,2,128]{2,4,3,1,0:T(8,128)(2,1)} %bitcast.126), kind=kOutput, calls=%fused_computation.19 | convolution fusion | flops 1094713344 | bytes 21790720 | tf_op jit(solution)/shard_map/srkgc,kscd->srkgd/dot_general | solution.py:25
  99.3 13.7 %fusion.5 = (f32[4,16,16]{2,1,0:T(8,128)}, f32[4,16,16]{2,1,0:T(8,128)}) fusion(f32[4,4096,16,16]{1,3,2,0:T(8,128)} %get-tuple-element.250, f32[4,16,16]{2,1,0:T(8,128)} %get-tuple-element.249, pred[4,16,4096]{2,1,0:T(8,128)(4,1)S(1)} %get-tuple-element.245, f32[4,16,16]{2,1,0:T(8,128)} %get-tuple-element.247, ...), kind=kLoop, calls=%fused_computation.14 | loop fusion | flops 41940992 | bytes 34095104 | tf_op jit(solution)/shard_map/reduce_sum | solution.py:24
  113.0 7.0 %fusion.12 = f32[4,16,16,128]{3,2,1,0:T(8,128)} fusion(f32[4,4096,16,16]{1,3,2,0:T(8,128)S(1)} %get-tuple-element.248, f32[4,16,16]{2,1,0:T(8,128)} %get-tuple-element.247, pred[4,16,4096]{2,1,0:T(8,128)(4,1)S(1)} %get-tuple-element.246, bf16[1,4,4096,2,128]{2,4,3,1,0:T(8,128)(2,1)} %bitcast.127), kind=kOutput, calls=%fused_computation.20 | convolution fusion | flops 1094713344 | bytes 21790720 | tf_op jit(solution)/shard_map/srkgc,kscd->srkgd/dot_general | solution.py:25
  121.6 183.3 %while.19 = (s32[]{:T(128)}, f32[2,2,1,16]{3,1,0,2:T(2,128)S(1)}, f32[2,2,1,16]{3,1,0,2:T(2,128)S(1)}, f32[2,2,1,16,128]{4,3,2,1,0:T(8,128)S(1)}, s32[]{:T(128)}...) while((s32[]{:T(128)}, f32[2,2,1,16]{3,1,0,2:T(2,128)S(1)}, ...), condition=%wide.region_5.6_spmd, body=%wide.region_4.5_spmd.sunk | while | flops 25042 | bytes 235184 | solution.py:91
  121.9 2.8 collective-permute-start
  125.5 2.2 collective-permute-done.1
  132.8 2.8 collective-permute-start
  136.5 2.2 collective-permute-done.1
  143.8 2.8 collective-permute-start
  147.4 2.2 collective-permute-done.1
  155.6 3.2 %collective-permute-start = (f32[2,2,1,16]{3,1,0,2:T(2,128)S(1)}, f32[2,2,1,16]{3,1,0,2:T(2,128)S(1)}, u32[]{:S(2)}, u32[]{:S(2)}) collective-permute-start(f32[2,2,1,16]{3,1,0,2:T(2,128)S(1)} %get-tuple-element.306), channel_id=1, source_target_pairs={{0,1},{1,2},{2,3},{3,4},{4,5},{5,6},{6,7},{7,8},{8,9},{9,10},{10,1... | collective-permute-start | bytes 776 | tf_op jit(solution)/shard_map/while/body/eval_jaxpr/ppermute | solution.py:12
  159.6 2.2 collective-permute-done.1
  162.0 2.9 collective-permute-start
  165.7 2.2 collective-permute-done.1
  168.2 2.5 collective-permute-start
  171.5 2.1 collective-permute-done.1
  173.9 2.5 collective-permute-start
  177.2 2.1 collective-permute-done.1
  179.6 2.5 collective-permute-start
  182.9 2.1 collective-permute-done.1
  185.3 2.5 collective-permute-start
  188.6 2.1 collective-permute-done.1
  191.0 2.5 collective-permute-start
  194.3 2.1 collective-permute-done.1
  196.7 2.5 collective-permute-start
  200.0 2.1 collective-permute-done.1
  202.4 2.5 collective-permute-start
  205.7 2.1 collective-permute-done.1
  208.1 2.5 collective-permute-start
  211.5 2.1 collective-permute-done.1
  213.8 2.5 collective-permute-start
  217.2 2.1 collective-permute-done.1
  219.5 2.5 collective-permute-start
  222.9 2.1 collective-permute-done.1
  225.2 2.5 collective-permute-start
  228.6 2.1 collective-permute-done.1
  230.9 2.5 collective-permute-start
  234.3 2.1 collective-permute-done.1
  236.6 2.5 collective-permute-start
  242.4 2.5 collective-permute-start
  245.7 2.1 collective-permute-done.1
  248.1 2.5 collective-permute-start
  251.4 2.1 collective-permute-done.1
  253.8 2.5 collective-permute-start
  257.1 2.1 collective-permute-done.1
  259.5 2.5 collective-permute-start
  262.8 2.1 collective-permute-done.1
  265.2 2.5 collective-permute-start
  268.5 2.1 collective-permute-done.1
  270.9 2.5 collective-permute-start
  274.2 2.1 collective-permute-done.1
  276.6 2.5 collective-permute-start
  282.3 2.5 collective-permute-start
  288.0 2.5 collective-permute-start
  293.7 2.5 collective-permute-start
  299.4 2.5 collective-permute-start
  (269 shorter events, 62.3 us)
Async XLA Ops:
  26.7 18.6 %all-to-all-start = ((bf16[8,2,16384]{2,1,0:T(2,128)(2,1)}), bf16[8,2,16384]{2,1,0:T(2,128)(2,1)S(1)}, u32[]{:S(2)}, u32[]{:S(2)}) async-start(bf16[8,2,16384]{2,1,0:T(2,128)(2,1)} %reshape.122), calls=%async_computation | async-start | bytes 1048576 | tf_op jit(solution)/shard_map/all_to_all | solution.py:44
  121.8 5.9 %collective-permute-start.2 = (f32[2,2,1,16,128]{4,3,2,1,0:T(8,128)S(1)}, f32[2,2,1,16,128]{4,3,2,1,0:T(8,128)S(1)}, u32[]{:S(2)}, u32[]{:S(2)}) collective-permute-start(f32[2,2,1,16,128]{4,3,2,1,0:T(8,128)S(1)} %multiply_add_fusion.3), channel_id=1, source_target_pairs={{0,1},{1,2},{2,3},{3,4},{4,5},{5,6},{6,7},{7,8},{8,9},{9,10},{10,1... | collective-permute-start | bytes 98312 | tf_op jit(solution)/shard_map/while/body/eval_jaxpr/ppermute | solution.py:12
  121.9 3.6 %collective-permute-start = (f32[2,2,1,16]{3,1,0,2:T(2,128)S(1)}, f32[2,2,1,16]{3,1,0,2:T(2,128)S(1)}, u32[]{:S(2)}, u32[]{:S(2)}) collective-permute-start(f32[2,2,1,16]{3,1,0,2:T(2,128)S(1)} %get-tuple-element.306), channel_id=1, source_target_pairs={{0,1},{1,2},{2,3},{3,4},{4,5},{5,6},{6,7},{7,8},{8,9},{9,10},{10,1... | collective-permute-start | bytes 776 | tf_op jit(solution)/shard_map/while/body/eval_jaxpr/ppermute | solution.py:12
  127.8 4.8 %collective-permute-start.2 = (f32[2,2,1,16,128]{4,3,2,1,0:T(8,128)S(1)}, f32[2,2,1,16,128]{4,3,2,1,0:T(8,128)S(1)}, u32[]{:S(2)}, u32[]{:S(2)}) collective-permute-start(f32[2,2,1,16,128]{4,3,2,1,0:T(8,128)S(1)} %multiply_add_fusion.3), channel_id=1, source_target_pairs={{0,1},{1,2},{2,3},{3,4},{4,5},{5,6},{6,7},{7,8},{8,9},{9,10},{10,1... | collective-permute-start | bytes 98312 | tf_op jit(solution)/shard_map/while/body/eval_jaxpr/ppermute | solution.py:12
  127.9 3.3 %collective-permute-start = (f32[2,2,1,16]{3,1,0,2:T(2,128)S(1)}, f32[2,2,1,16]{3,1,0,2:T(2,128)S(1)}, u32[]{:S(2)}, u32[]{:S(2)}) collective-permute-start(f32[2,2,1,16]{3,1,0,2:T(2,128)S(1)} %get-tuple-element.306), channel_id=1, source_target_pairs={{0,1},{1,2},{2,3},{3,4},{4,5},{5,6},{6,7},{7,8},{8,9},{9,10},{10,1... | collective-permute-start | bytes 776 | tf_op jit(solution)/shard_map/while/body/eval_jaxpr/ppermute | solution.py:12
  132.8 5.9 %collective-permute-start.2 = (f32[2,2,1,16,128]{4,3,2,1,0:T(8,128)S(1)}, f32[2,2,1,16,128]{4,3,2,1,0:T(8,128)S(1)}, u32[]{:S(2)}, u32[]{:S(2)}) collective-permute-start(f32[2,2,1,16,128]{4,3,2,1,0:T(8,128)S(1)} %multiply_add_fusion.3), channel_id=1, source_target_pairs={{0,1},{1,2},{2,3},{3,4},{4,5},{5,6},{6,7},{7,8},{8,9},{9,10},{10,1... | collective-permute-start | bytes 98312 | tf_op jit(solution)/shard_map/while/body/eval_jaxpr/ppermute | solution.py:12
  132.8 3.6 %collective-permute-start = (f32[2,2,1,16]{3,1,0,2:T(2,128)S(1)}, f32[2,2,1,16]{3,1,0,2:T(2,128)S(1)}, u32[]{:S(2)}, u32[]{:S(2)}) collective-permute-start(f32[2,2,1,16]{3,1,0,2:T(2,128)S(1)} %get-tuple-element.306), channel_id=1, source_target_pairs={{0,1},{1,2},{2,3},{3,4},{4,5},{5,6},{6,7},{7,8},{8,9},{9,10},{10,1... | collective-permute-start | bytes 776 | tf_op jit(solution)/shard_map/while/body/eval_jaxpr/ppermute | solution.py:12
  138.8 4.8 %collective-permute-start.2 = (f32[2,2,1,16,128]{4,3,2,1,0:T(8,128)S(1)}, f32[2,2,1,16,128]{4,3,2,1,0:T(8,128)S(1)}, u32[]{:S(2)}, u32[]{:S(2)}) collective-permute-start(f32[2,2,1,16,128]{4,3,2,1,0:T(8,128)S(1)} %multiply_add_fusion.3), channel_id=1, source_target_pairs={{0,1},{1,2},{2,3},{3,4},{4,5},{5,6},{6,7},{7,8},{8,9},{9,10},{10,1... | collective-permute-start | bytes 98312 | tf_op jit(solution)/shard_map/while/body/eval_jaxpr/ppermute | solution.py:12
  138.9 3.3 %collective-permute-start = (f32[2,2,1,16]{3,1,0,2:T(2,128)S(1)}, f32[2,2,1,16]{3,1,0,2:T(2,128)S(1)}, u32[]{:S(2)}, u32[]{:S(2)}) collective-permute-start(f32[2,2,1,16]{3,1,0,2:T(2,128)S(1)} %get-tuple-element.306), channel_id=1, source_target_pairs={{0,1},{1,2},{2,3},{3,4},{4,5},{5,6},{6,7},{7,8},{8,9},{9,10},{10,1... | collective-permute-start | bytes 776 | tf_op jit(solution)/shard_map/while/body/eval_jaxpr/ppermute | solution.py:12
  143.7 5.9 %collective-permute-start.2 = (f32[2,2,1,16,128]{4,3,2,1,0:T(8,128)S(1)}, f32[2,2,1,16,128]{4,3,2,1,0:T(8,128)S(1)}, u32[]{:S(2)}, u32[]{:S(2)}) collective-permute-start(f32[2,2,1,16,128]{4,3,2,1,0:T(8,128)S(1)} %multiply_add_fusion.3), channel_id=1, source_target_pairs={{0,1},{1,2},{2,3},{3,4},{4,5},{5,6},{6,7},{7,8},{8,9},{9,10},{10,1... | collective-permute-start | bytes 98312 | tf_op jit(solution)/shard_map/while/body/eval_jaxpr/ppermute | solution.py:12
  143.8 3.6 %collective-permute-start = (f32[2,2,1,16]{3,1,0,2:T(2,128)S(1)}, f32[2,2,1,16]{3,1,0,2:T(2,128)S(1)}, u32[]{:S(2)}, u32[]{:S(2)}) collective-permute-start(f32[2,2,1,16]{3,1,0,2:T(2,128)S(1)} %get-tuple-element.306), channel_id=1, source_target_pairs={{0,1},{1,2},{2,3},{3,4},{4,5},{5,6},{6,7},{7,8},{8,9},{9,10},{10,1... | collective-permute-start | bytes 776 | tf_op jit(solution)/shard_map/while/body/eval_jaxpr/ppermute | solution.py:12
  149.8 4.8 %collective-permute-start.2 = (f32[2,2,1,16,128]{4,3,2,1,0:T(8,128)S(1)}, f32[2,2,1,16,128]{4,3,2,1,0:T(8,128)S(1)}, u32[]{:S(2)}, u32[]{:S(2)}) collective-permute-start(f32[2,2,1,16,128]{4,3,2,1,0:T(8,128)S(1)} %multiply_add_fusion.3), channel_id=1, source_target_pairs={{0,1},{1,2},{2,3},{3,4},{4,5},{5,6},{6,7},{7,8},{8,9},{9,10},{10,1... | collective-permute-start | bytes 98312 | tf_op jit(solution)/shard_map/while/body/eval_jaxpr/ppermute | solution.py:12
  149.8 3.3 %collective-permute-start = (f32[2,2,1,16]{3,1,0,2:T(2,128)S(1)}, f32[2,2,1,16]{3,1,0,2:T(2,128)S(1)}, u32[]{:S(2)}, u32[]{:S(2)}) collective-permute-start(f32[2,2,1,16]{3,1,0,2:T(2,128)S(1)} %get-tuple-element.306), channel_id=1, source_target_pairs={{0,1},{1,2},{2,3},{3,4},{4,5},{5,6},{6,7},{7,8},{8,9},{9,10},{10,1... | collective-permute-start | bytes 776 | tf_op jit(solution)/shard_map/while/body/eval_jaxpr/ppermute | solution.py:12
  154.7 7.1 %collective-permute-start.2 = (f32[2,2,1,16,128]{4,3,2,1,0:T(8,128)S(1)}, f32[2,2,1,16,128]{4,3,2,1,0:T(8,128)S(1)}, u32[]{:S(2)}, u32[]{:S(2)}) collective-permute-start(f32[2,2,1,16,128]{4,3,2,1,0:T(8,128)S(1)} %multiply_add_fusion.3), channel_id=1, source_target_pairs={{0,1},{1,2},{2,3},{3,4},{4,5},{5,6},{6,7},{7,8},{8,9},{9,10},{10,1... | collective-permute-start | bytes 98312 | tf_op jit(solution)/shard_map/while/body/eval_jaxpr/ppermute | solution.py:12
  155.6 4.0 %collective-permute-start = (f32[2,2,1,16]{3,1,0,2:T(2,128)S(1)}, f32[2,2,1,16]{3,1,0,2:T(2,128)S(1)}, u32[]{:S(2)}, u32[]{:S(2)}) collective-permute-start(f32[2,2,1,16]{3,1,0,2:T(2,128)S(1)} %get-tuple-element.306), channel_id=1, source_target_pairs={{0,1},{1,2},{2,3},{3,4},{4,5},{5,6},{6,7},{7,8},{8,9},{9,10},{10,1... | collective-permute-start | bytes 776 | tf_op jit(solution)/shard_map/while/body/eval_jaxpr/ppermute | solution.py:12
  161.9 6.0 %collective-permute-start.2 = (f32[2,2,1,16,128]{4,3,2,1,0:T(8,128)S(1)}, f32[2,2,1,16,128]{4,3,2,1,0:T(8,128)S(1)}, u32[]{:S(2)}, u32[]{:S(2)}) collective-permute-start(f32[2,2,1,16,128]{4,3,2,1,0:T(8,128)S(1)} %multiply_add_fusion.3), channel_id=1, source_target_pairs={{0,1},{1,2},{2,3},{3,4},{4,5},{5,6},{6,7},{7,8},{8,9},{9,10},{10,1... | collective-permute-start | bytes 98312 | tf_op jit(solution)/shard_map/while/body/eval_jaxpr/ppermute | solution.py:12
  162.0 3.7 %collective-permute-start = (f32[2,2,1,16]{3,1,0,2:T(2,128)S(1)}, f32[2,2,1,16]{3,1,0,2:T(2,128)S(1)}, u32[]{:S(2)}, u32[]{:S(2)}) collective-permute-start(f32[2,2,1,16]{3,1,0,2:T(2,128)S(1)} %get-tuple-element.306), channel_id=1, source_target_pairs={{0,1},{1,2},{2,3},{3,4},{4,5},{5,6},{6,7},{7,8},{8,9},{9,10},{10,1... | collective-permute-start | bytes 776 | tf_op jit(solution)/shard_map/while/body/eval_jaxpr/ppermute | solution.py:12
  168.1 5.6 %collective-permute-start.2 = (f32[2,2,1,16,128]{4,3,2,1,0:T(8,128)S(1)}, f32[2,2,1,16,128]{4,3,2,1,0:T(8,128)S(1)}, u32[]{:S(2)}, u32[]{:S(2)}) collective-permute-start(f32[2,2,1,16,128]{4,3,2,1,0:T(8,128)S(1)} %multiply_add_fusion.3), channel_id=1, source_target_pairs={{0,1},{1,2},{2,3},{3,4},{4,5},{5,6},{6,7},{7,8},{8,9},{9,10},{10,1... | collective-permute-start | bytes 98312 | tf_op jit(solution)/shard_map/while/body/eval_jaxpr/ppermute | solution.py:12
  168.2 3.3 %collective-permute-start = (f32[2,2,1,16]{3,1,0,2:T(2,128)S(1)}, f32[2,2,1,16]{3,1,0,2:T(2,128)S(1)}, u32[]{:S(2)}, u32[]{:S(2)}) collective-permute-start(f32[2,2,1,16]{3,1,0,2:T(2,128)S(1)} %get-tuple-element.306), channel_id=1, source_target_pairs={{0,1},{1,2},{2,3},{3,4},{4,5},{5,6},{6,7},{7,8},{8,9},{9,10},{10,1... | collective-permute-start | bytes 776 | tf_op jit(solution)/shard_map/while/body/eval_jaxpr/ppermute | solution.py:12
  173.8 5.6 %collective-permute-start.2 = (f32[2,2,1,16,128]{4,3,2,1,0:T(8,128)S(1)}, f32[2,2,1,16,128]{4,3,2,1,0:T(8,128)S(1)}, u32[]{:S(2)}, u32[]{:S(2)}) collective-permute-start(f32[2,2,1,16,128]{4,3,2,1,0:T(8,128)S(1)} %multiply_add_fusion.3), channel_id=1, source_target_pairs={{0,1},{1,2},{2,3},{3,4},{4,5},{5,6},{6,7},{7,8},{8,9},{9,10},{10,1... | collective-permute-start | bytes 98312 | tf_op jit(solution)/shard_map/while/body/eval_jaxpr/ppermute | solution.py:12
  173.9 3.3 %collective-permute-start = (f32[2,2,1,16]{3,1,0,2:T(2,128)S(1)}, f32[2,2,1,16]{3,1,0,2:T(2,128)S(1)}, u32[]{:S(2)}, u32[]{:S(2)}) collective-permute-start(f32[2,2,1,16]{3,1,0,2:T(2,128)S(1)} %get-tuple-element.306), channel_id=1, source_target_pairs={{0,1},{1,2},{2,3},{3,4},{4,5},{5,6},{6,7},{7,8},{8,9},{9,10},{10,1... | collective-permute-start | bytes 776 | tf_op jit(solution)/shard_map/while/body/eval_jaxpr/ppermute | solution.py:12
  179.5 5.6 %collective-permute-start.2 = (f32[2,2,1,16,128]{4,3,2,1,0:T(8,128)S(1)}, f32[2,2,1,16,128]{4,3,2,1,0:T(8,128)S(1)}, u32[]{:S(2)}, u32[]{:S(2)}) collective-permute-start(f32[2,2,1,16,128]{4,3,2,1,0:T(8,128)S(1)} %multiply_add_fusion.3), channel_id=1, source_target_pairs={{0,1},{1,2},{2,3},{3,4},{4,5},{5,6},{6,7},{7,8},{8,9},{9,10},{10,1... | collective-permute-start | bytes 98312 | tf_op jit(solution)/shard_map/while/body/eval_jaxpr/ppermute | solution.py:12
  179.6 3.3 %collective-permute-start = (f32[2,2,1,16]{3,1,0,2:T(2,128)S(1)}, f32[2,2,1,16]{3,1,0,2:T(2,128)S(1)}, u32[]{:S(2)}, u32[]{:S(2)}) collective-permute-start(f32[2,2,1,16]{3,1,0,2:T(2,128)S(1)} %get-tuple-element.306), channel_id=1, source_target_pairs={{0,1},{1,2},{2,3},{3,4},{4,5},{5,6},{6,7},{7,8},{8,9},{9,10},{10,1... | collective-permute-start | bytes 776 | tf_op jit(solution)/shard_map/while/body/eval_jaxpr/ppermute | solution.py:12
  185.2 5.6 %collective-permute-start.2 = (f32[2,2,1,16,128]{4,3,2,1,0:T(8,128)S(1)}, f32[2,2,1,16,128]{4,3,2,1,0:T(8,128)S(1)}, u32[]{:S(2)}, u32[]{:S(2)}) collective-permute-start(f32[2,2,1,16,128]{4,3,2,1,0:T(8,128)S(1)} %multiply_add_fusion.3), channel_id=1, source_target_pairs={{0,1},{1,2},{2,3},{3,4},{4,5},{5,6},{6,7},{7,8},{8,9},{9,10},{10,1... | collective-permute-start | bytes 98312 | tf_op jit(solution)/shard_map/while/body/eval_jaxpr/ppermute | solution.py:12
  185.3 3.3 %collective-permute-start = (f32[2,2,1,16]{3,1,0,2:T(2,128)S(1)}, f32[2,2,1,16]{3,1,0,2:T(2,128)S(1)}, u32[]{:S(2)}, u32[]{:S(2)}) collective-permute-start(f32[2,2,1,16]{3,1,0,2:T(2,128)S(1)} %get-tuple-element.306), channel_id=1, source_target_pairs={{0,1},{1,2},{2,3},{3,4},{4,5},{5,6},{6,7},{7,8},{8,9},{9,10},{10,1... | collective-permute-start | bytes 776 | tf_op jit(solution)/shard_map/while/body/eval_jaxpr/ppermute | solution.py:12
  190.9 5.6 %collective-permute-start.2 = (f32[2,2,1,16,128]{4,3,2,1,0:T(8,128)S(1)}, f32[2,2,1,16,128]{4,3,2,1,0:T(8,128)S(1)}, u32[]{:S(2)}, u32[]{:S(2)}) collective-permute-start(f32[2,2,1,16,128]{4,3,2,1,0:T(8,128)S(1)} %multiply_add_fusion.3), channel_id=1, source_target_pairs={{0,1},{1,2},{2,3},{3,4},{4,5},{5,6},{6,7},{7,8},{8,9},{9,10},{10,1... | collective-permute-start | bytes 98312 | tf_op jit(solution)/shard_map/while/body/eval_jaxpr/ppermute | solution.py:12
  191.0 3.3 %collective-permute-start = (f32[2,2,1,16]{3,1,0,2:T(2,128)S(1)}, f32[2,2,1,16]{3,1,0,2:T(2,128)S(1)}, u32[]{:S(2)}, u32[]{:S(2)}) collective-permute-start(f32[2,2,1,16]{3,1,0,2:T(2,128)S(1)} %get-tuple-element.306), channel_id=1, source_target_pairs={{0,1},{1,2},{2,3},{3,4},{4,5},{5,6},{6,7},{7,8},{8,9},{9,10},{10,1... | collective-permute-start | bytes 776 | tf_op jit(solution)/shard_map/while/body/eval_jaxpr/ppermute | solution.py:12
  196.6 5.6 %collective-permute-start.2 = (f32[2,2,1,16,128]{4,3,2,1,0:T(8,128)S(1)}, f32[2,2,1,16,128]{4,3,2,1,0:T(8,128)S(1)}, u32[]{:S(2)}, u32[]{:S(2)}) collective-permute-start(f32[2,2,1,16,128]{4,3,2,1,0:T(8,128)S(1)} %multiply_add_fusion.3), channel_id=1, source_target_pairs={{0,1},{1,2},{2,3},{3,4},{4,5},{5,6},{6,7},{7,8},{8,9},{9,10},{10,1... | collective-permute-start | bytes 98312 | tf_op jit(solution)/shard_map/while/body/eval_jaxpr/ppermute | solution.py:12
  196.7 3.3 %collective-permute-start = (f32[2,2,1,16]{3,1,0,2:T(2,128)S(1)}, f32[2,2,1,16]{3,1,0,2:T(2,128)S(1)}, u32[]{:S(2)}, u32[]{:S(2)}) collective-permute-start(f32[2,2,1,16]{3,1,0,2:T(2,128)S(1)} %get-tuple-element.306), channel_id=1, source_target_pairs={{0,1},{1,2},{2,3},{3,4},{4,5},{5,6},{6,7},{7,8},{8,9},{9,10},{10,1... | collective-permute-start | bytes 776 | tf_op jit(solution)/shard_map/while/body/eval_jaxpr/ppermute | solution.py:12
  202.3 5.6 %collective-permute-start.2 = (f32[2,2,1,16,128]{4,3,2,1,0:T(8,128)S(1)}, f32[2,2,1,16,128]{4,3,2,1,0:T(8,128)S(1)}, u32[]{:S(2)}, u32[]{:S(2)}) collective-permute-start(f32[2,2,1,16,128]{4,3,2,1,0:T(8,128)S(1)} %multiply_add_fusion.3), channel_id=1, source_target_pairs={{0,1},{1,2},{2,3},{3,4},{4,5},{5,6},{6,7},{7,8},{8,9},{9,10},{10,1... | collective-permute-start | bytes 98312 | tf_op jit(solution)/shard_map/while/body/eval_jaxpr/ppermute | solution.py:12
  202.4 3.3 %collective-permute-start = (f32[2,2,1,16]{3,1,0,2:T(2,128)S(1)}, f32[2,2,1,16]{3,1,0,2:T(2,128)S(1)}, u32[]{:S(2)}, u32[]{:S(2)}) collective-permute-start(f32[2,2,1,16]{3,1,0,2:T(2,128)S(1)} %get-tuple-element.306), channel_id=1, source_target_pairs={{0,1},{1,2},{2,3},{3,4},{4,5},{5,6},{6,7},{7,8},{8,9},{9,10},{10,1... | collective-permute-start | bytes 776 | tf_op jit(solution)/shard_map/while/body/eval_jaxpr/ppermute | solution.py:12
  208.0 5.6 %collective-permute-start.2 = (f32[2,2,1,16,128]{4,3,2,1,0:T(8,128)S(1)}, f32[2,2,1,16,128]{4,3,2,1,0:T(8,128)S(1)}, u32[]{:S(2)}, u32[]{:S(2)}) collective-permute-start(f32[2,2,1,16,128]{4,3,2,1,0:T(8,128)S(1)} %multiply_add_fusion.3), channel_id=1, source_target_pairs={{0,1},{1,2},{2,3},{3,4},{4,5},{5,6},{6,7},{7,8},{8,9},{9,10},{10,1... | collective-permute-start | bytes 98312 | tf_op jit(solution)/shard_map/while/body/eval_jaxpr/ppermute | solution.py:12
  208.1 3.3 %collective-permute-start = (f32[2,2,1,16]{3,1,0,2:T(2,128)S(1)}, f32[2,2,1,16]{3,1,0,2:T(2,128)S(1)}, u32[]{:S(2)}, u32[]{:S(2)}) collective-permute-start(f32[2,2,1,16]{3,1,0,2:T(2,128)S(1)} %get-tuple-element.306), channel_id=1, source_target_pairs={{0,1},{1,2},{2,3},{3,4},{4,5},{5,6},{6,7},{7,8},{8,9},{9,10},{10,1... | collective-permute-start | bytes 776 | tf_op jit(solution)/shard_map/while/body/eval_jaxpr/ppermute | solution.py:12
  213.7 5.6 %collective-permute-start.2 = (f32[2,2,1,16,128]{4,3,2,1,0:T(8,128)S(1)}, f32[2,2,1,16,128]{4,3,2,1,0:T(8,128)S(1)}, u32[]{:S(2)}, u32[]{:S(2)}) collective-permute-start(f32[2,2,1,16,128]{4,3,2,1,0:T(8,128)S(1)} %multiply_add_fusion.3), channel_id=1, source_target_pairs={{0,1},{1,2},{2,3},{3,4},{4,5},{5,6},{6,7},{7,8},{8,9},{9,10},{10,1... | collective-permute-start | bytes 98312 | tf_op jit(solution)/shard_map/while/body/eval_jaxpr/ppermute | solution.py:12
  213.8 3.3 %collective-permute-start = (f32[2,2,1,16]{3,1,0,2:T(2,128)S(1)}, f32[2,2,1,16]{3,1,0,2:T(2,128)S(1)}, u32[]{:S(2)}, u32[]{:S(2)}) collective-permute-start(f32[2,2,1,16]{3,1,0,2:T(2,128)S(1)} %get-tuple-element.306), channel_id=1, source_target_pairs={{0,1},{1,2},{2,3},{3,4},{4,5},{5,6},{6,7},{7,8},{8,9},{9,10},{10,1... | collective-permute-start | bytes 776 | tf_op jit(solution)/shard_map/while/body/eval_jaxpr/ppermute | solution.py:12
  219.4 5.6 %collective-permute-start.2 = (f32[2,2,1,16,128]{4,3,2,1,0:T(8,128)S(1)}, f32[2,2,1,16,128]{4,3,2,1,0:T(8,128)S(1)}, u32[]{:S(2)}, u32[]{:S(2)}) collective-permute-start(f32[2,2,1,16,128]{4,3,2,1,0:T(8,128)S(1)} %multiply_add_fusion.3), channel_id=1, source_target_pairs={{0,1},{1,2},{2,3},{3,4},{4,5},{5,6},{6,7},{7,8},{8,9},{9,10},{10,1... | collective-permute-start | bytes 98312 | tf_op jit(solution)/shard_map/while/body/eval_jaxpr/ppermute | solution.py:12
  219.5 3.3 %collective-permute-start = (f32[2,2,1,16]{3,1,0,2:T(2,128)S(1)}, f32[2,2,1,16]{3,1,0,2:T(2,128)S(1)}, u32[]{:S(2)}, u32[]{:S(2)}) collective-permute-start(f32[2,2,1,16]{3,1,0,2:T(2,128)S(1)} %get-tuple-element.306), channel_id=1, source_target_pairs={{0,1},{1,2},{2,3},{3,4},{4,5},{5,6},{6,7},{7,8},{8,9},{9,10},{10,1... | collective-permute-start | bytes 776 | tf_op jit(solution)/shard_map/while/body/eval_jaxpr/ppermute | solution.py:12
  225.1 5.6 %collective-permute-start.2 = (f32[2,2,1,16,128]{4,3,2,1,0:T(8,128)S(1)}, f32[2,2,1,16,128]{4,3,2,1,0:T(8,128)S(1)}, u32[]{:S(2)}, u32[]{:S(2)}) collective-permute-start(f32[2,2,1,16,128]{4,3,2,1,0:T(8,128)S(1)} %multiply_add_fusion.3), channel_id=1, source_target_pairs={{0,1},{1,2},{2,3},{3,4},{4,5},{5,6},{6,7},{7,8},{8,9},{9,10},{10,1... | collective-permute-start | bytes 98312 | tf_op jit(solution)/shard_map/while/body/eval_jaxpr/ppermute | solution.py:12
  225.2 3.3 %collective-permute-start = (f32[2,2,1,16]{3,1,0,2:T(2,128)S(1)}, f32[2,2,1,16]{3,1,0,2:T(2,128)S(1)}, u32[]{:S(2)}, u32[]{:S(2)}) collective-permute-start(f32[2,2,1,16]{3,1,0,2:T(2,128)S(1)} %get-tuple-element.306), channel_id=1, source_target_pairs={{0,1},{1,2},{2,3},{3,4},{4,5},{5,6},{6,7},{7,8},{8,9},{9,10},{10,1... | collective-permute-start | bytes 776 | tf_op jit(solution)/shard_map/while/body/eval_jaxpr/ppermute | solution.py:12
  230.8 5.6 %collective-permute-start.2 = (f32[2,2,1,16,128]{4,3,2,1,0:T(8,128)S(1)}, f32[2,2,1,16,128]{4,3,2,1,0:T(8,128)S(1)}, u32[]{:S(2)}, u32[]{:S(2)}) collective-permute-start(f32[2,2,1,16,128]{4,3,2,1,0:T(8,128)S(1)} %multiply_add_fusion.3), channel_id=1, source_target_pairs={{0,1},{1,2},{2,3},{3,4},{4,5},{5,6},{6,7},{7,8},{8,9},{9,10},{10,1... | collective-permute-start | bytes 98312 | tf_op jit(solution)/shard_map/while/body/eval_jaxpr/ppermute | solution.py:12
  230.9 3.3 %collective-permute-start = (f32[2,2,1,16]{3,1,0,2:T(2,128)S(1)}, f32[2,2,1,16]{3,1,0,2:T(2,128)S(1)}, u32[]{:S(2)}, u32[]{:S(2)}) collective-permute-start(f32[2,2,1,16]{3,1,0,2:T(2,128)S(1)} %get-tuple-element.306), channel_id=1, source_target_pairs={{0,1},{1,2},{2,3},{3,4},{4,5},{5,6},{6,7},{7,8},{8,9},{9,10},{10,1... | collective-permute-start | bytes 776 | tf_op jit(solution)/shard_map/while/body/eval_jaxpr/ppermute | solution.py:12
  236.6 5.6 %collective-permute-start.2 = (f32[2,2,1,16,128]{4,3,2,1,0:T(8,128)S(1)}, f32[2,2,1,16,128]{4,3,2,1,0:T(8,128)S(1)}, u32[]{:S(2)}, u32[]{:S(2)}) collective-permute-start(f32[2,2,1,16,128]{4,3,2,1,0:T(8,128)S(1)} %multiply_add_fusion.3), channel_id=1, source_target_pairs={{0,1},{1,2},{2,3},{3,4},{4,5},{5,6},{6,7},{7,8},{8,9},{9,10},{10,1... | collective-permute-start | bytes 98312 | tf_op jit(solution)/shard_map/while/body/eval_jaxpr/ppermute | solution.py:12
  236.6 3.3 %collective-permute-start = (f32[2,2,1,16]{3,1,0,2:T(2,128)S(1)}, f32[2,2,1,16]{3,1,0,2:T(2,128)S(1)}, u32[]{:S(2)}, u32[]{:S(2)}) collective-permute-start(f32[2,2,1,16]{3,1,0,2:T(2,128)S(1)} %get-tuple-element.306), channel_id=1, source_target_pairs={{0,1},{1,2},{2,3},{3,4},{4,5},{5,6},{6,7},{7,8},{8,9},{9,10},{10,1... | collective-permute-start | bytes 776 | tf_op jit(solution)/shard_map/while/body/eval_jaxpr/ppermute | solution.py:12
  242.3 5.6 %collective-permute-start.2 = (f32[2,2,1,16,128]{4,3,2,1,0:T(8,128)S(1)}, f32[2,2,1,16,128]{4,3,2,1,0:T(8,128)S(1)}, u32[]{:S(2)}, u32[]{:S(2)}) collective-permute-start(f32[2,2,1,16,128]{4,3,2,1,0:T(8,128)S(1)} %multiply_add_fusion.3), channel_id=1, source_target_pairs={{0,1},{1,2},{2,3},{3,4},{4,5},{5,6},{6,7},{7,8},{8,9},{9,10},{10,1... | collective-permute-start | bytes 98312 | tf_op jit(solution)/shard_map/while/body/eval_jaxpr/ppermute | solution.py:12
  242.4 3.3 %collective-permute-start = (f32[2,2,1,16]{3,1,0,2:T(2,128)S(1)}, f32[2,2,1,16]{3,1,0,2:T(2,128)S(1)}, u32[]{:S(2)}, u32[]{:S(2)}) collective-permute-start(f32[2,2,1,16]{3,1,0,2:T(2,128)S(1)} %get-tuple-element.306), channel_id=1, source_target_pairs={{0,1},{1,2},{2,3},{3,4},{4,5},{5,6},{6,7},{7,8},{8,9},{9,10},{10,1... | collective-permute-start | bytes 776 | tf_op jit(solution)/shard_map/while/body/eval_jaxpr/ppermute | solution.py:12
  248.0 5.6 %collective-permute-start.2 = (f32[2,2,1,16,128]{4,3,2,1,0:T(8,128)S(1)}, f32[2,2,1,16,128]{4,3,2,1,0:T(8,128)S(1)}, u32[]{:S(2)}, u32[]{:S(2)}) collective-permute-start(f32[2,2,1,16,128]{4,3,2,1,0:T(8,128)S(1)} %multiply_add_fusion.3), channel_id=1, source_target_pairs={{0,1},{1,2},{2,3},{3,4},{4,5},{5,6},{6,7},{7,8},{8,9},{9,10},{10,1... | collective-permute-start | bytes 98312 | tf_op jit(solution)/shard_map/while/body/eval_jaxpr/ppermute | solution.py:12
  248.1 3.3 %collective-permute-start = (f32[2,2,1,16]{3,1,0,2:T(2,128)S(1)}, f32[2,2,1,16]{3,1,0,2:T(2,128)S(1)}, u32[]{:S(2)}, u32[]{:S(2)}) collective-permute-start(f32[2,2,1,16]{3,1,0,2:T(2,128)S(1)} %get-tuple-element.306), channel_id=1, source_target_pairs={{0,1},{1,2},{2,3},{3,4},{4,5},{5,6},{6,7},{7,8},{8,9},{9,10},{10,1... | collective-permute-start | bytes 776 | tf_op jit(solution)/shard_map/while/body/eval_jaxpr/ppermute | solution.py:12
  253.7 5.6 %collective-permute-start.2 = (f32[2,2,1,16,128]{4,3,2,1,0:T(8,128)S(1)}, f32[2,2,1,16,128]{4,3,2,1,0:T(8,128)S(1)}, u32[]{:S(2)}, u32[]{:S(2)}) collective-permute-start(f32[2,2,1,16,128]{4,3,2,1,0:T(8,128)S(1)} %multiply_add_fusion.3), channel_id=1, source_target_pairs={{0,1},{1,2},{2,3},{3,4},{4,5},{5,6},{6,7},{7,8},{8,9},{9,10},{10,1... | collective-permute-start | bytes 98312 | tf_op jit(solution)/shard_map/while/body/eval_jaxpr/ppermute | solution.py:12
  253.8 3.3 %collective-permute-start = (f32[2,2,1,16]{3,1,0,2:T(2,128)S(1)}, f32[2,2,1,16]{3,1,0,2:T(2,128)S(1)}, u32[]{:S(2)}, u32[]{:S(2)}) collective-permute-start(f32[2,2,1,16]{3,1,0,2:T(2,128)S(1)} %get-tuple-element.306), channel_id=1, source_target_pairs={{0,1},{1,2},{2,3},{3,4},{4,5},{5,6},{6,7},{7,8},{8,9},{9,10},{10,1... | collective-permute-start | bytes 776 | tf_op jit(solution)/shard_map/while/body/eval_jaxpr/ppermute | solution.py:12
  259.4 5.6 %collective-permute-start.2 = (f32[2,2,1,16,128]{4,3,2,1,0:T(8,128)S(1)}, f32[2,2,1,16,128]{4,3,2,1,0:T(8,128)S(1)}, u32[]{:S(2)}, u32[]{:S(2)}) collective-permute-start(f32[2,2,1,16,128]{4,3,2,1,0:T(8,128)S(1)} %multiply_add_fusion.3), channel_id=1, source_target_pairs={{0,1},{1,2},{2,3},{3,4},{4,5},{5,6},{6,7},{7,8},{8,9},{9,10},{10,1... | collective-permute-start | bytes 98312 | tf_op jit(solution)/shard_map/while/body/eval_jaxpr/ppermute | solution.py:12
  259.5 3.3 %collective-permute-start = (f32[2,2,1,16]{3,1,0,2:T(2,128)S(1)}, f32[2,2,1,16]{3,1,0,2:T(2,128)S(1)}, u32[]{:S(2)}, u32[]{:S(2)}) collective-permute-start(f32[2,2,1,16]{3,1,0,2:T(2,128)S(1)} %get-tuple-element.306), channel_id=1, source_target_pairs={{0,1},{1,2},{2,3},{3,4},{4,5},{5,6},{6,7},{7,8},{8,9},{9,10},{10,1... | collective-permute-start | bytes 776 | tf_op jit(solution)/shard_map/while/body/eval_jaxpr/ppermute | solution.py:12
  265.1 5.6 %collective-permute-start.2 = (f32[2,2,1,16,128]{4,3,2,1,0:T(8,128)S(1)}, f32[2,2,1,16,128]{4,3,2,1,0:T(8,128)S(1)}, u32[]{:S(2)}, u32[]{:S(2)}) collective-permute-start(f32[2,2,1,16,128]{4,3,2,1,0:T(8,128)S(1)} %multiply_add_fusion.3), channel_id=1, source_target_pairs={{0,1},{1,2},{2,3},{3,4},{4,5},{5,6},{6,7},{7,8},{8,9},{9,10},{10,1... | collective-permute-start | bytes 98312 | tf_op jit(solution)/shard_map/while/body/eval_jaxpr/ppermute | solution.py:12
  265.2 3.3 %collective-permute-start = (f32[2,2,1,16]{3,1,0,2:T(2,128)S(1)}, f32[2,2,1,16]{3,1,0,2:T(2,128)S(1)}, u32[]{:S(2)}, u32[]{:S(2)}) collective-permute-start(f32[2,2,1,16]{3,1,0,2:T(2,128)S(1)} %get-tuple-element.306), channel_id=1, source_target_pairs={{0,1},{1,2},{2,3},{3,4},{4,5},{5,6},{6,7},{7,8},{8,9},{9,10},{10,1... | collective-permute-start | bytes 776 | tf_op jit(solution)/shard_map/while/body/eval_jaxpr/ppermute | solution.py:12
  270.8 5.6 %collective-permute-start.2 = (f32[2,2,1,16,128]{4,3,2,1,0:T(8,128)S(1)}, f32[2,2,1,16,128]{4,3,2,1,0:T(8,128)S(1)}, u32[]{:S(2)}, u32[]{:S(2)}) collective-permute-start(f32[2,2,1,16,128]{4,3,2,1,0:T(8,128)S(1)} %multiply_add_fusion.3), channel_id=1, source_target_pairs={{0,1},{1,2},{2,3},{3,4},{4,5},{5,6},{6,7},{7,8},{8,9},{9,10},{10,1... | collective-permute-start | bytes 98312 | tf_op jit(solution)/shard_map/while/body/eval_jaxpr/ppermute | solution.py:12
  270.9 3.3 %collective-permute-start = (f32[2,2,1,16]{3,1,0,2:T(2,128)S(1)}, f32[2,2,1,16]{3,1,0,2:T(2,128)S(1)}, u32[]{:S(2)}, u32[]{:S(2)}) collective-permute-start(f32[2,2,1,16]{3,1,0,2:T(2,128)S(1)} %get-tuple-element.306), channel_id=1, source_target_pairs={{0,1},{1,2},{2,3},{3,4},{4,5},{5,6},{6,7},{7,8},{8,9},{9,10},{10,1... | collective-permute-start | bytes 776 | tf_op jit(solution)/shard_map/while/body/eval_jaxpr/ppermute | solution.py:12
  276.5 5.6 %collective-permute-start.2 = (f32[2,2,1,16,128]{4,3,2,1,0:T(8,128)S(1)}, f32[2,2,1,16,128]{4,3,2,1,0:T(8,128)S(1)}, u32[]{:S(2)}, u32[]{:S(2)}) collective-permute-start(f32[2,2,1,16,128]{4,3,2,1,0:T(8,128)S(1)} %multiply_add_fusion.3), channel_id=1, source_target_pairs={{0,1},{1,2},{2,3},{3,4},{4,5},{5,6},{6,7},{7,8},{8,9},{9,10},{10,1... | collective-permute-start | bytes 98312 | tf_op jit(solution)/shard_map/while/body/eval_jaxpr/ppermute | solution.py:12
  276.6 3.3 %collective-permute-start = (f32[2,2,1,16]{3,1,0,2:T(2,128)S(1)}, f32[2,2,1,16]{3,1,0,2:T(2,128)S(1)}, u32[]{:S(2)}, u32[]{:S(2)}) collective-permute-start(f32[2,2,1,16]{3,1,0,2:T(2,128)S(1)} %get-tuple-element.306), channel_id=1, source_target_pairs={{0,1},{1,2},{2,3},{3,4},{4,5},{5,6},{6,7},{7,8},{8,9},{9,10},{10,1... | collective-permute-start | bytes 776 | tf_op jit(solution)/shard_map/while/body/eval_jaxpr/ppermute | solution.py:12
  282.2 5.6 %collective-permute-start.2 = (f32[2,2,1,16,128]{4,3,2,1,0:T(8,128)S(1)}, f32[2,2,1,16,128]{4,3,2,1,0:T(8,128)S(1)}, u32[]{:S(2)}, u32[]{:S(2)}) collective-permute-start(f32[2,2,1,16,128]{4,3,2,1,0:T(8,128)S(1)} %multiply_add_fusion.3), channel_id=1, source_target_pairs={{0,1},{1,2},{2,3},{3,4},{4,5},{5,6},{6,7},{7,8},{8,9},{9,10},{10,1... | collective-permute-start | bytes 98312 | tf_op jit(solution)/shard_map/while/body/eval_jaxpr/ppermute | solution.py:12
  282.3 3.3 %collective-permute-start = (f32[2,2,1,16]{3,1,0,2:T(2,128)S(1)}, f32[2,2,1,16]{3,1,0,2:T(2,128)S(1)}, u32[]{:S(2)}, u32[]{:S(2)}) collective-permute-start(f32[2,2,1,16]{3,1,0,2:T(2,128)S(1)} %get-tuple-element.306), channel_id=1, source_target_pairs={{0,1},{1,2},{2,3},{3,4},{4,5},{5,6},{6,7},{7,8},{8,9},{9,10},{10,1... | collective-permute-start | bytes 776 | tf_op jit(solution)/shard_map/while/body/eval_jaxpr/ppermute | solution.py:12
  287.9 5.6 %collective-permute-start.2 = (f32[2,2,1,16,128]{4,3,2,1,0:T(8,128)S(1)}, f32[2,2,1,16,128]{4,3,2,1,0:T(8,128)S(1)}, u32[]{:S(2)}, u32[]{:S(2)}) collective-permute-start(f32[2,2,1,16,128]{4,3,2,1,0:T(8,128)S(1)} %multiply_add_fusion.3), channel_id=1, source_target_pairs={{0,1},{1,2},{2,3},{3,4},{4,5},{5,6},{6,7},{7,8},{8,9},{9,10},{10,1... | collective-permute-start | bytes 98312 | tf_op jit(solution)/shard_map/while/body/eval_jaxpr/ppermute | solution.py:12
  288.0 3.3 %collective-permute-start = (f32[2,2,1,16]{3,1,0,2:T(2,128)S(1)}, f32[2,2,1,16]{3,1,0,2:T(2,128)S(1)}, u32[]{:S(2)}, u32[]{:S(2)}) collective-permute-start(f32[2,2,1,16]{3,1,0,2:T(2,128)S(1)} %get-tuple-element.306), channel_id=1, source_target_pairs={{0,1},{1,2},{2,3},{3,4},{4,5},{5,6},{6,7},{7,8},{8,9},{9,10},{10,1... | collective-permute-start | bytes 776 | tf_op jit(solution)/shard_map/while/body/eval_jaxpr/ppermute | solution.py:12
  293.6 5.6 %collective-permute-start.2 = (f32[2,2,1,16,128]{4,3,2,1,0:T(8,128)S(1)}, f32[2,2,1,16,128]{4,3,2,1,0:T(8,128)S(1)}, u32[]{:S(2)}, u32[]{:S(2)}) collective-permute-start(f32[2,2,1,16,128]{4,3,2,1,0:T(8,128)S(1)} %multiply_add_fusion.3), channel_id=1, source_target_pairs={{0,1},{1,2},{2,3},{3,4},{4,5},{5,6},{6,7},{7,8},{8,9},{9,10},{10,1... | collective-permute-start | bytes 98312 | tf_op jit(solution)/shard_map/while/body/eval_jaxpr/ppermute | solution.py:12
  293.7 3.3 %collective-permute-start = (f32[2,2,1,16]{3,1,0,2:T(2,128)S(1)}, f32[2,2,1,16]{3,1,0,2:T(2,128)S(1)}, u32[]{:S(2)}, u32[]{:S(2)}) collective-permute-start(f32[2,2,1,16]{3,1,0,2:T(2,128)S(1)} %get-tuple-element.306), channel_id=1, source_target_pairs={{0,1},{1,2},{2,3},{3,4},{4,5},{5,6},{6,7},{7,8},{8,9},{9,10},{10,1... | collective-permute-start | bytes 776 | tf_op jit(solution)/shard_map/while/body/eval_jaxpr/ppermute | solution.py:12
  299.3 5.6 %collective-permute-start.2 = (f32[2,2,1,16,128]{4,3,2,1,0:T(8,128)S(1)}, f32[2,2,1,16,128]{4,3,2,1,0:T(8,128)S(1)}, u32[]{:S(2)}, u32[]{:S(2)}) collective-permute-start(f32[2,2,1,16,128]{4,3,2,1,0:T(8,128)S(1)} %multiply_add_fusion.3), channel_id=1, source_target_pairs={{0,1},{1,2},{2,3},{3,4},{4,5},{5,6},{6,7},{7,8},{8,9},{9,10},{10,1... | collective-permute-start | bytes 98312 | tf_op jit(solution)/shard_map/while/body/eval_jaxpr/ppermute | solution.py:12
  (38 other events, 161.5 us)
where the time goes:
time: 310 us; the launch traced here: 306 us
  waiting for transfers between devices  92.7 us (30%)
  starting transfers between devices  92.5 us (30%)
  local copies, waits for them, and re-layouts  68.2 us (22%)
  matrix products  32.2 us (10%)
  other arithmetic  19 us (6%)
    ppermute x96, waiting for transfers between devices, from_behind(): return lax.ppermute(value, axis, pairs)  92.7 us
    ppermute x96, starting transfers between devices, from_behind(): return lax.ppermute(value, axis, pairs)  86 us
    unnamed x17, local copies, waits for them, and re-layouts  49.3 us
    all_to_all x1, local copies, waits for them, and re-layouts, shards(): lax.all_to_all(queries, 'kv', split_axis=2, concat_axis=1, tiled=True)  17.7 us
    dot_general x2, matrix products, shard_terms(): jnp.einsum('srkgc,kscd->srkgd', weights.astype(jnp.bfloat16), cached_valu...  16.2 us
    dot_general x2, matrix products, shard_terms(): jnp.einsum('srkgd,kscd->srkgc', rollout_queries, cached_keys, preferred_e...  16 us
    reduce_sum x1, other arithmetic, shard_terms(): row_sum = jnp.sum(weights, axis=-1)  13.7 us
    all_to_all x1, starting transfers between devices, shards(): lax.all_to_all(queries, 'kv', split_axis=2, concat_axis=1, tiled=True)  6.53 us
  transfers between devices with their start and end apart: 97, of which 64 were waited for; matrix products, arithmetic and copies ran while one was open for 4% of the time, Pallas kernels for 0%

commit v1 on v0

v1 whole, which is shorter than its diff:
```python
import functools

import jax
import jax.numpy as jnp
from jax import lax
from jax.experimental import pallas as pl
from jax.experimental.pallas import tpu as pltpu
from jax.sharding import PartitionSpec as P

F32, BF16 = jnp.float32, jnp.bfloat16
STEPS, ROWS, GROUP, HEAD = 2, 64, 16, 128
UNITS, PROMPTS, SPAN = 8, 4, 4096
UNIT_ROWS = STEPS * (ROWS // UNITS) * GROUP
SCALE = 1.4426950408889634 / HEAD**0.5
HIDE = 2.0**20
CHUNK = 1024


def nt(a, b):
    return lax.dot_general(a, b, (((1,), (1,)), ((), ())), preferred_element_type=F32)


def limit_lanes(lengths_ref):
    lane = lax.broadcasted_iota(jnp.int32, (8, 128), 1)
    row = lane % ROWS
    held = jnp.zeros((8, 128), jnp.int32)
    for r in range(ROWS):
        held = jnp.where(row == r, lengths_ref[r], held)
    return held + lane // ROWS


def attend(lengths_ref, q_ref, kv_hbm, o_ref, lse_ref, kv, hide, s0, s1, sems):
    scores = (s0, s1)
    for p in range(PROMPTS):
        pltpu.make_async_copy(kv_hbm.at[0, p], kv.at[p], sems.at[p]).start()
    limits = limit_lanes(lengths_ref) - lax.axis_index("ctx") * SPAN

    def fill(i, _):
        position = lax.broadcasted_iota(jnp.int32, (64, 128), 0) + i * 64
        at = pl.ds(pl.multiple_of(i * 64, 64), 64)
        hide[at, :] = jnp.where(position < limits[0:1, :], 0.0, -HIDE).astype(BF16)
        return 0

    lax.fori_loop(0, SPAN // 64, fill, 0)

    def wait(p):
        pltpu.make_async_copy(kv_hbm.at[0, p], kv.at[p], sems.at[p]).wait()

    def marked(u):
        i = lax.broadcasted_iota(jnp.int32, (UNIT_ROWS, 128), 0)
        lane = lax.broadcasted_iota(jnp.int32, (UNIT_ROWS, 128), 1)
        target = (i // 128) * ROWS + u * 8 + (i % 128) // GROUP
        return jnp.concatenate([q_ref[u], (lane == target).astype(BF16)], axis=1)

    ones = jnp.ones((CHUNK, 128), BF16)

    def stage(u, n, use, make, top):
        if u is not None:
            peak = jnp.max(top, axis=1, keepdims=True) * SCALE
            total = None
        if n is not None:
            q = marked(n)
            new_top = None
        for c in range(SPAN // CHUNK):
            at = slice(c * CHUNK, (c + 1) * CHUNK)
            if n is not None:
                k = jnp.concatenate([kv[n // 2, at, 0:HEAD], hide[at, :]], axis=1)
                s = nt(q, k)
                scores[make][:, at] = s
                for b in range(CHUNK // 128):
                    x = s[:, b * 128 : (b + 1) * 128]
                    new_top = x if new_top is None else jnp.maximum(new_top, x)
            if u is not None:
                w = jnp.exp2(scores[use][:, at] * SCALE - peak).astype(BF16)
                v = jnp.concatenate([kv[u // 2, at, HEAD : 2 * HEAD], ones], axis=1)
                part = jnp.dot(w, v, preferred_element_type=F32)
                total = part if total is None else total + part
        if u is not None:
            weight = total[:, HEAD:]
            o = (total[:, :HEAD] / weight).astype(BF16)
            lse = jnp.log2(weight) + peak
            for d in range(4):
                for t in range(STEPS):
                    src = slice(t * 128 + d * 32, t * 128 + d * 32 + 32)
                    o_ref[4 * u + d, t * 32 : t * 32 + 32, :] = o[src, :]
                    lse_ref[4 * u + d, t * 32 : t * 32 + 32, :] = lse[src, :]
        return new_top if n is not None else None

    wait(0)
    top = stage(None, 0, 1, 0, None)

    def pair(i, top):
        u = i * 2
        top = stage(u, u + 1, 0, 1, top)
        wait(i + 1)
        return stage(u + 1, u + 2, 1, 0, top)

    top = lax.fori_loop(0, UNITS // 2 - 1, pair, top)
    top = stage(UNITS - 2, UNITS - 1, 0, 1, top)
    stage(UNITS - 1, None, 1, None, top)


def shards(queries, kv_cache, lengths):
    sent = queries.reshape(STEPS, 8, 8, GROUP, HEAD).transpose(2, 0, 1, 3, 4)
    held = lax.all_to_all(sent, "kv", split_axis=0, concat_axis=0)
    held = held.reshape(UNITS, UNIT_ROWS, HEAD)
    o, lse = pl.pallas_call(
        attend,
        out_shape=[
            jax.ShapeDtypeStruct((32, 64, HEAD), BF16),
            jax.ShapeDtypeStruct((32, 64, HEAD), F32),
        ],
        in_specs=[
            pl.BlockSpec(memory_space=pltpu.SMEM),
            pl.BlockSpec(memory_space=pltpu.VMEM),
            pl.BlockSpec(memory_space=pl.ANY),
        ],
        out_specs=[pl.BlockSpec(memory_space=pltpu.VMEM)] * 2,
        scratch_shapes=[
            pltpu.VMEM((PROMPTS, SPAN, 2 * HEAD), BF16),
            pltpu.VMEM((SPAN, 128), BF16),
            pltpu.VMEM((UNIT_ROWS, SPAN), F32),
            pltpu.VMEM((UNIT_ROWS, SPAN), F32),
            pltpu.SemaphoreType.DMA((PROMPTS,)),
        ],
        compiler_params=pltpu.CompilerParams(vmem_limit_bytes=50 * 2**20),
        name="attend",
    )(lengths, held, kv_cache)
    o = lax.all_to_all(o, "ctx", split_axis=0, concat_axis=0)
    lse = lax.all_to_all(lse[:, :, 0], "ctx", split_axis=0, concat_axis=0)
    factor = jnp.exp2(lse - jnp.max(lse, axis=0, keepdims=True))
    total = jnp.sum(factor, axis=0)[:, None]
    out = jnp.sum(o.astype(F32) * factor[:, :, None], axis=0) / total
    return out.astype(BF16).reshape(STEPS, 2, GROUP * HEAD)


def solution(mesh):
    in_specs = (P(None, "kv", None), P("kv", None, "ctx", None), P())
    out_specs = P(None, "ctx", "kv")
    return jax.shard_map(shards, mesh=mesh, in_specs=in_specs, out_specs=out_specs, check_vma=False)
```

time: 310 us -> 74.6 us (0.24)
  the two profiles are of different devices: /device:TPU:12 before, /device:TPU:1 now
where the time goes in v1:
time: 74.6 us; the launch traced here: 74.3 us
  blocking collectives  35.9 us (48%)
  waiting for transfers between devices  16.8 us (23%)
  Pallas kernels  14 us (19%)
  starting transfers between devices  4.15 us (6%)
  local copies, waits for them, and re-layouts  2.35 us (3%)
  other arithmetic  1.05 us (1%)
    all_to_all x1, blocking collectives, shards(): lse = lax.all_to_all(lse[:, :, 0], 'ctx', split_axis=0, concat_axis=0)  19 us
    all_to_all x1, blocking collectives, shards(): held = lax.all_to_all(sent, 'kv', split_axis=0, concat_axis=0)  16.9 us
    all_to_all x1, waiting for transfers between devices, shards(): o = lax.all_to_all(o, 'ctx', split_axis=0, concat_axis=0)  16.8 us
    pallas_call x1, Pallas kernels, shards(): pl.pallas_call(attend, out_shape=[jax.ShapeDtypeStruct((32, 64, HEAD), BF...  14 us
    all_to_all x1, starting transfers between devices, shards(): o = lax.all_to_all(o, 'ctx', split_axis=0, concat_axis=0)  4.15 us
  transfers between devices with their start and end apart: 1, of which 1 were waited for; matrix products, arithmetic and copies ran while one was open for 0% of the time, Pallas kernels for 0%

profile of v1, /device:TPU:1, one launch (start us, length us, event | category | flops | bytes accessed | tf_op | source)
XLA Modules:
  0.0 74.3 jit_solution(3685077474239654221)
XLA Ops:
  0.0 1.1 %copy.9 = bf16[2,8,8,16,128]{4,3,1,0,2:T(8,128)(2,1)S(1)} copy(bf16[2,8,8,16,128]{4,1,3,2,0:T(8,128)(2,1)} %bitcast.13) | data formatting | bytes 1048576 | tf_op jit(solution)/shard_map/reshape | solution.py:104
  1.2 16.9 %all_to_all.22 = bf16[8,2,8,16,128]{4,3,2,1,0:T(8,128)(2,1)S(1)} all-to-all(bf16[8,2,8,16,128]{4,3,2,1,0:T(8,128)(2,1)S(1)} %bitcast.12), channel_id=1, replica_groups=mesh['kv'=8,'ctx'=32] {'kv'}, dimensions={0} | all-to-all | bytes 1048576 | tf_op jit(solution)/shard_map/all_to_all | solution.py:105
  18.0 0.0 copy-start
  18.0 0.7 copy-done
  18.7 14.0 %attend.1 = (bf16[32,64,128]{2,1,0:T(8,128)(2,1)}, f32[32,64,128]{2,1,0:T(8,128)S(1)}) custom-call(s32[64]{0:T(128)S(1)} %copy-done, bf16[8,256,128]{2,1,0:T(8,128)(2,1)S(1)} %bitcast.11, bf16[1,4,4096,256]{3,2,1,0:T(8,128)(2,1)} %kv_hbm.1), custom_call_target="tpu_custom_call" | custom-call | tf_op jit(solution)/shard_map/attend/pallas_call | solution.py:107
  32.7 0.3 slice_reduce_fusion
  33.0 19.0 %all_to_all.23 = f32[32,1,64]{2,1,0:T(1,128)S(1)} all-to-all(f32[32,1,64]{2,1,0:T(1,128)S(1)} %bitcast.15), channel_id=1, replica_groups=mesh['kv'=8,'ctx'=32] {'ctx'}, dimensions={0} | all-to-all | bytes 16384 | tf_op jit(solution)/shard_map/all_to_all | solution.py:130
  52.0 4.2 %all-to-all-start.1 = ((bf16[32,64,128]{2,1,0:T(8,128)(2,1)}), bf16[32,64,128]{2,1,0:T(8,128)(2,1)S(1)}, u32[]{:S(2)}, u32[]{:S(2)}) async-start(bf16[32,64,128]{2,1,0:T(8,128)(2,1)} %get-tuple-element.7), calls=%async_computation.1 | async-start | bytes 1048576 | tf_op jit(solution)/shard_map/all_to_all | solution.py:129
  56.2 0.1 reduce_max.9
  56.3 0.1 div.13
  56.4 0.1 div.14
  56.5 16.8 %all-to-all-done.1 = bf16[32,64,128]{2,1,0:T(8,128)(2,1)S(1)} async-done(((bf16[32,64,128]{2,1,0:T(8,128)(2,1)}), bf16[32,64,128]{2,1,0:T(8,128)(2,1)S(1)}, u32[]{:S(2)}, u32[]{:S(2)}) %all-to-all-start.1) | async-done | bytes 524320 | tf_op jit(solution)/shard_map/all_to_all | solution.py:129
  73.3 0.3 multiply_reduce_fusion
  73.6 0.6 divide_convert_fusion
  (3 shorter events, 0.1 us)
Async XLA Ops:
  18.0 0.7 copy-start
  52.0 21.2 %all-to-all-start.1 = ((bf16[32,64,128]{2,1,0:T(8,128)(2,1)}), bf16[32,64,128]{2,1,0:T(8,128)(2,1)S(1)}, u32[]{:S(2)}, u32[]{:S(2)}) async-start(bf16[32,64,128]{2,1,0:T(8,128)(2,1)} %get-tuple-element.7), calls=%async_computation.1 | async-start | bytes 1048576 | tf_op jit(solution)/shard_map/all_to_all | solution.py:129

commit v2 on v1

v2 whole, which is shorter than its diff:
```python
import jax
import jax.numpy as jnp
from jax import lax
from jax.experimental import pallas as pl
from jax.experimental.pallas import tpu as pltpu
from jax.sharding import PartitionSpec as P

F32, BF16 = jnp.float32, jnp.bfloat16
STEPS, ROWS, GROUP, HEAD = 2, 64, 16, 128
UNITS, PROMPTS, SPAN = 8, 4, 4096
UNIT_ROWS = STEPS * (ROWS // UNITS) * GROUP
PART = UNIT_ROWS // 4
BLOCK = PART + 16
SCALE = 1.4426950408889634 / HEAD**0.5
HIDE = 2.0**20
CHUNK = 1024
MESH = pl.DeviceIdType.MESH


def nt(a, b):
    return lax.dot_general(a, b, (((1,), (1,)), ((), ())), preferred_element_type=F32)


def limit_lanes(lengths_ref):
    lane = lax.broadcasted_iota(jnp.int32, (8, 128), 1)
    row = lane % ROWS
    held = jnp.zeros((8, 128), jnp.int32)
    for r in range(ROWS):
        held = jnp.where(row == r, lengths_ref[r], held)
    return held + lane // ROWS


def pack(lse, base):
    rows = lse[0].shape[0]
    sub = lax.broadcasted_iota(jnp.int32, (rows, 128), 0)
    lane = lax.broadcasted_iota(jnp.int32, (rows, 128), 1)
    at = lax.broadcasted_iota(jnp.int32, (16, 128), 0)
    tile = jnp.zeros((16, 128), F32)
    for t in range(STEPS):
        x = jnp.sum(jnp.where(lane == sub + base, lse[t], 0.0), axis=0, keepdims=True)
        high = x.astype(BF16).astype(F32)
        rest = x - high
        middle = rest.astype(BF16).astype(F32)
        for k, term in enumerate((high, middle, rest - middle)):
            tile = jnp.where(at == 2 * k + t, term, tile)
    return tile.astype(BF16)


def unpack(block, base):
    o = block[0:PART].astype(F32)
    tile = block[PART:BLOCK].astype(F32)
    half = PART // STEPS
    sub = lax.broadcasted_iota(jnp.int32, (half, 128), 0)
    lane = lax.broadcasted_iota(jnp.int32, (half, 128), 1)
    lse = []
    for t in range(STEPS):
        x = tile[t : t + 1] + tile[2 + t : 3 + t] + tile[4 + t : 5 + t]
        spread = jnp.where(lane == sub + base, jnp.broadcast_to(x, (half, 128)), 0.0)
        lse.append(jnp.sum(spread, axis=1, keepdims=True))
    return o, jnp.concatenate(lse, axis=0)


def merge(parts):
    top = parts[0][1]
    for _, lse in parts[1:]:
        top = jnp.maximum(top, lse)
    total, weighted = None, None
    for o, lse in parts:
        factor = jnp.exp2(lse - top)
        total = factor if total is None else total + factor
        weighted = o * factor if weighted is None else weighted + o * factor
    return weighted / total, jnp.log2(total) + top


def attend(
    lengths_ref, q_hbm, kv_hbm, out_ref,
    kv, qs, hide, s0, s1, psend, precv, zsend, zrecv,
    kv_sem, own_sem, q_out, q_in, p_out, p_in, z_out, z_in,
):
    scores = (s0, s1)
    me = lax.axis_index("kv")
    ctx = lax.axis_index("ctx")
    plane = ctx // 4
    place = ctx % 4
    flip = 2 - 4 * (place // 2)
    last = (plane - me + UNITS) % UNITS
    base = place * (PART // STEPS)

    def unit_at(i):
        after = jnp.where(i >= last, i + 1, i)
        return (me + after) % UNITS

    def wait_kv(p):
        pltpu.make_async_copy(kv_hbm.at[0, p], kv.at[p], kv_sem.at[p]).wait()

    def query_copy(k, source):
        across = (k + me) % 2
        return pltpu.make_async_remote_copy(
            src_ref=q_hbm.at[k],
            dst_ref=qs.at[source],
            send_sem=q_out.at[k],
            recv_sem=q_in.at[source],
            device_id=(k, ctx + across * flip),
            device_id_type=MESH,
        )

    def plane_copy(i, o):
        there = (place + o) % 4
        return pltpu.make_async_remote_copy(
            src_ref=psend.at[i, there],
            dst_ref=precv.at[i, o - 1],
            send_sem=p_out.at[i, o - 1],
            recv_sem=p_in.at[i, o - 1],
            device_id=(me, plane * 4 + there),
            device_id_type=MESH,
        )

    def z_copy(i, z):
        return pltpu.make_async_remote_copy(
            src_ref=zsend.at[i],
            dst_ref=zrecv.at[plane],
            send_sem=z_out.at[i],
            recv_sem=z_in.at[plane],
            device_id=(me, z * 4 + place),
            device_id_type=MESH,
        )

    first = unit_at(0)
    for n in range(PROMPTS):
        p = (first // 2 + n) % PROMPTS
        pltpu.make_async_copy(kv_hbm.at[0, p], kv.at[p], kv_sem.at[p]).start()
    own = pltpu.make_async_copy(q_hbm.at[me], qs.at[me], own_sem)
    own.start()

    barrier = pltpu.get_barrier_semaphore()
    for n in range(1, UNITS):
        k = (me + n) % UNITS
        across = (k + me) % 2
        pl.semaphore_signal(barrier, inc=1, device_id=(k, ctx + across * flip), device_id_type=MESH)
        z = (plane + n) % UNITS
        pl.semaphore_signal(barrier, inc=1, device_id=(me, z * 4 + place), device_id_type=MESH)
    for o in range(1, 4):
        there = plane * 4 + (place + o) % 4
        pl.semaphore_signal(barrier, inc=1, device_id=(me, there), device_id_type=MESH)

    limits = limit_lanes(lengths_ref) - ctx * SPAN

    def fill(i, _):
        position = lax.broadcasted_iota(jnp.int32, (64, 128), 0) + i * 64
        at = pl.ds(pl.multiple_of(i * 64, 64), 64)
        hide[at, :] = jnp.where(position < limits[0:1, :], 0.0, -HIDE).astype(BF16)
        return 0

    lax.fori_loop(0, SPAN // 64, fill, 0)

    pl.semaphore_wait(barrier, 2 * (UNITS - 1) + 3)
    for n in range(1, UNITS):
        query_copy((me - n + UNITS) % UNITS, me).start()
    own.wait()

    def ready(i, u):
        @pl.when(u != me)
        def _():
            query_copy(u, u).wait_recv()

        mate = (u + 1 - 2 * (u % 2) - me + UNITS) % UNITS
        mate_at = jnp.where(mate == last, UNITS - 1, jnp.where(mate > last, mate - 1, mate))

        @pl.when(mate_at > i)
        def _():
            wait_kv(u // 2)

    def marked(u):
        i = lax.broadcasted_iota(jnp.int32, (UNIT_ROWS, 128), 0)
        lane = lax.broadcasted_iota(jnp.int32, (UNIT_ROWS, 128), 1)
        target = (i // 128) * ROWS + u * 8 + (i % 128) // GROUP
        return jnp.concatenate([qs[u], (lane == target).astype(BF16)], axis=1)

    ones = jnp.ones((CHUNK, 128), BF16)

    def stage(i, u, n, use, make, top):
        if u is not None:
            peak = jnp.max(top, axis=1, keepdims=True) * SCALE
            total = None
        if n is not None:
            q = marked(n)
            new_top = None
        for c in range(SPAN // CHUNK):
            at = slice(c * CHUNK, (c + 1) * CHUNK)
            if n is not None:
                k = jnp.concatenate([kv[n // 2, at, 0:HEAD], hide[at, :]], axis=1)
                s = nt(q, k)
                scores[make][:, at] = s
                for b in range(CHUNK // 128):
                    x = s[:, b * 128 : (b + 1) * 128]
                    new_top = x if new_top is None else jnp.maximum(new_top, x)
            if u is not None:
                w = jnp.exp2(scores[use][:, at] * SCALE - peak).astype(BF16)
                v = jnp.concatenate([kv[u // 2, at, HEAD : 2 * HEAD], ones], axis=1)
                part = jnp.dot(w, v, preferred_element_type=F32)
                total = part if total is None else total + part
        if u is not None:
            weight = total[:, HEAD:]
            o = (total[:, :HEAD] / weight).astype(BF16)
            lse = jnp.log2(weight) + peak
            sums = pack((lse[:128], lse[128:]), 0)
            for d in range(4):
                psend[i, d, 0:32, :] = o[d * 32 : d * 32 + 32]
                psend[i, d, 32:64, :] = o[128 + d * 32 : 160 + d * 32]
                psend[i, d, PART:BLOCK, :] = sums
        return new_top if n is not None else None

    def send_plane(i):
        for o in range(1, 4):
            plane_copy(i, o).start()

    def gather_plane(i):
        parts = [unpack(psend[i, place], base)]
        for o in range(1, 4):
            plane_copy(i, o).wait_recv()
            parts.append(unpack(precv[i, o - 1], base))
        return merge(parts)

    def pass_on(i):
        o, lse = gather_plane(i)
        half = PART // STEPS
        zsend[i, 0:PART, :] = o.astype(BF16)
        zsend[i, PART:BLOCK, :] = pack((lse[:half], lse[half:]), base)
        z_copy(i, unit_at(i)).start()

    ready(0, first)
    top = stage(0, None, first, 1, 0, None)

    def pair(h, top):
        i = 2 * h
        a, b, c = unit_at(i), unit_at(i + 1), unit_at(i + 2)
        ready(i + 1, b)
        top = stage(i, a, b, 0, 1, top)
        send_plane(i)

        @pl.when(h > 0)
        def _():
            pass_on(i - 1)

        ready(i + 2, c)
        top = stage(i + 1, b, c, 1, 0, top)
        send_plane(i + 1)
        pass_on(i)
        return top

    top = lax.fori_loop(0, UNITS // 2 - 1, pair, top)
    ready(UNITS - 1, plane)
    top = stage(UNITS - 2, unit_at(UNITS - 2), plane, 0, 1, top)
    send_plane(UNITS - 2)
    pass_on(UNITS - 3)
    stage(UNITS - 1, plane, None, 1, None, top)
    send_plane(UNITS - 1)
    pass_on(UNITS - 2)
    parts = [gather_plane(UNITS - 1)]
    for n in range(1, UNITS):
        z = (plane + n) % UNITS
        pltpu.make_async_remote_copy(
            src_ref=zsend.at[0],
            dst_ref=zrecv.at[z],
            send_sem=z_out.at[0],
            recv_sem=z_in.at[z],
            device_id=(me, z * 4 + place),
            device_id_type=MESH,
        ).wait_recv()
        parts.append(unpack(zrecv[z], base))
    out_ref[...] = merge(parts)[0].astype(BF16)

    for n in range(1, UNITS):
        query_copy((me - n + UNITS) % UNITS, me).wait_send()

    def sent(i, _):
        for o in range(1, 4):
            plane_copy(i, o).wait_send()
        return 0

    lax.fori_loop(0, UNITS, sent, 0)

    def sent_z(i, _):
        z_copy(i, unit_at(i)).wait_send()
        return 0

    lax.fori_loop(0, UNITS - 1, sent_z, 0)


def shards(queries, kv_cache, lengths):
    sent = queries.reshape(STEPS, 8, 8, GROUP, HEAD).transpose(2, 0, 1, 3, 4)
    out = pl.pallas_call(
        attend,
        out_shape=jax.ShapeDtypeStruct((PART, HEAD), BF16),
        in_specs=[
            pl.BlockSpec(memory_space=pltpu.SMEM),
            pl.BlockSpec(memory_space=pl.ANY),
            pl.BlockSpec(memory_space=pl.ANY),
        ],
        out_specs=pl.BlockSpec(memory_space=pltpu.VMEM),
        scratch_shapes=[
            pltpu.VMEM((PROMPTS, SPAN, 2 * HEAD), BF16),
            pltpu.VMEM((UNITS, UNIT_ROWS, HEAD), BF16),
            pltpu.VMEM((SPAN, 128), BF16),
            pltpu.VMEM((UNIT_ROWS, SPAN), F32),
            pltpu.VMEM((UNIT_ROWS, SPAN), F32),
            pltpu.VMEM((UNITS, 4, BLOCK, HEAD), BF16),
            pltpu.VMEM((UNITS, 3, BLOCK, HEAD), BF16),
            pltpu.VMEM((UNITS, BLOCK, HEAD), BF16),
            pltpu.VMEM((UNITS, BLOCK, HEAD), BF16),
            pltpu.SemaphoreType.DMA((PROMPTS,)),
            pltpu.SemaphoreType.DMA,
            pltpu.SemaphoreType.DMA((UNITS,)),
            pltpu.SemaphoreType.DMA((UNITS,)),
            pltpu.SemaphoreType.DMA((UNITS, 3)),
            pltpu.SemaphoreType.DMA((UNITS, 3)),
            pltpu.SemaphoreType.DMA((UNITS,)),
            pltpu.SemaphoreType.DMA((UNITS,)),
        ],
        compiler_params=pltpu.CompilerParams(
            vmem_limit_bytes=50 * 2**20, collective_id=0, has_side_effects=True
        ),
        name="attend",
    )(lengths, sent.reshape(UNITS, UNIT_ROWS, HEAD), kv_cache)
    return out.reshape(STEPS, 2, GROUP * HEAD)


def solution(mesh):
    in_specs = (P(None, "kv", None), P("kv", None, "ctx", None), P())
    out_specs = P(None, "ctx", "kv")
    return jax.shard_map(shards, mesh=mesh, in_specs=in_specs, out_specs=out_specs, check_vma=False)
```

time: 74.6 us -> 41 us (0.55)
  the two profiles are of different devices: /device:TPU:1 before, /device:TPU:24 now
where the time goes in v2:
time: 41 us; the launch traced here: 40.8 us
  Pallas kernels  38.4 us (94%)
  local copies, waits for them, and re-layouts  2.41 us (6%)
    pallas_call x1, Pallas kernels, shards(): pl.pallas_call(attend, out_shape=jax.ShapeDtypeStruct((PART, HEAD), BF16)...  38.4 us
    reshape x1, local copies, waits for them, and re-layouts, shards(): sent = queries.reshape(STEPS, 8, 8, GROUP, HEAD).transpose(2, 0, 1, 3, 4)  1.14 us

profile of v2, /device:TPU:24, one launch (start us, length us, event | category | flops | bytes accessed | tf_op | source)
XLA Modules:
  0.0 40.8 jit_solution(9910771894100464268)
XLA Ops:
  0.0 1.1 %copy.4 = bf16[2,8,8,16,128]{4,3,1,0,2:T(8,128)(2,1)S(1)} copy(bf16[2,8,8,16,128]{4,1,3,2,0:T(8,128)(2,1)} %bitcast.5) | data formatting | bytes 1048576 | tf_op jit(solution)/shard_map/reshape | solution.py:291
  1.2 0.0 copy-start
  1.2 0.6 %copy-done = s32[64]{0:T(128)S(1)} copy-done((s32[64]{0:T(128)S(1)}, s32[64]{0:T(128)}, u32[]{:S(2)}) %copy-start) | copy-done | bytes 280
  1.8 38.4 %attend.1 = bf16[64,128]{1,0:T(8,128)(2,1)S(1)} custom-call(s32[64]{0:T(128)S(1)} %copy-done, bf16[8,256,128]{2,1,0:T(8,128)(2,1)S(1)} %bitcast.4, bf16[1,4,4096,256]{3,2,1,0:T(8,128)(2,1)} %kv_hbm.1), custom_call_target="tpu_custom_call" | custom-call | tf_op jit(solution)/shard_map/attend/pallas_call | solution.py:292
  40.2 0.6 %reshape.11 = bf16[2,2,2048]{2,1,0:T(2,128)(2,1)} reshape(bf16[64,128]{1,0:T(8,128)(2,1)S(1)} %attend.1) | data formatting | bytes 32768 | tf_op jit(solution)/shard_map/reshape | solution.py:325
Async XLA Ops:
  1.2 0.7 %copy-start = (s32[64]{0:T(128)S(1)}, s32[64]{0:T(128)}, u32[]{:S(2)}) copy-start(s32[64]{0:T(128)} %lengths_ref.1) | copy-start | bytes 772

commit v3 on v2

v3 whole, which is shorter than its diff:
```python
import jax
import jax.numpy as jnp
from jax import lax
from jax.experimental import pallas as pl
from jax.experimental.pallas import tpu as pltpu
from jax.sharding import PartitionSpec as P

F32, BF16 = jnp.float32, jnp.bfloat16
STEPS, ROWS, GROUP, HEAD = 2, 64, 16, 128
UNITS, PROMPTS, SPAN = 8, 4, 4096
WIDE = GROUP * HEAD
UNIT_ROWS = STEPS * GROUP * (ROWS // UNITS)
PART = UNIT_ROWS // 4
BLOCK = PART + 16
SCALE = 1.4426950408889634 / HEAD**0.5
HIDE = 2.0**20
CHUNK = 1024
MESH = pl.DeviceIdType.MESH


def nt(a, b):
    return lax.dot_general(a, b, (((1,), (1,)), ((), ())), preferred_element_type=F32)


def limit_lanes(lengths_ref):
    lane = lax.broadcasted_iota(jnp.int32, (8, 128), 1)
    row = lane % ROWS
    held = jnp.zeros((8, 128), jnp.int32)
    for r in range(ROWS):
        held = jnp.where(row == r, lengths_ref[r], held)
    return held + lane // ROWS


def pack(lse):
    sub = lax.broadcasted_iota(jnp.int32, (128, 128), 0)
    lane = lax.broadcasted_iota(jnp.int32, (128, 128), 1)
    at = lax.broadcasted_iota(jnp.int32, (16, 128), 0)
    tile = jnp.zeros((16, 128), F32)
    for t in range(STEPS):
        x = jnp.sum(jnp.where(lane == sub, lse[t], 0.0), axis=0, keepdims=True)
        high = x.astype(BF16).astype(F32)
        rest = x - high
        middle = rest.astype(BF16).astype(F32)
        for k, term in enumerate((high, middle, rest - middle)):
            tile = jnp.where(at == 2 * k + t, term, tile)
    return tile.astype(BF16)


def lane_of(place, e):
    sub = lax.broadcasted_iota(jnp.int32, (GROUP, 128), 0)
    lane = lax.broadcasted_iota(jnp.int32, (GROUP, 128), 1)
    return lane == sub * 8 + 2 * place + e


def pack_part(lse, place):
    at = lax.broadcasted_iota(jnp.int32, (16, 128), 0)
    tile = jnp.zeros((16, 128), F32)
    for t in range(STEPS):
        spread = jnp.zeros((GROUP, 128), F32)
        for e in range(2):
            k = e * 32 + t * 16
            spread = jnp.where(lane_of(place, e), lse[k : k + 16], spread)
        x = jnp.sum(spread, axis=0, keepdims=True)
        high = x.astype(BF16).astype(F32)
        rest = x - high
        middle = rest.astype(BF16).astype(F32)
        for k, term in enumerate((high, middle, rest - middle)):
            tile = jnp.where(at == 2 * k + t, term, tile)
    return tile.astype(BF16)


def unpack(block, place):
    o = block[0:PART].astype(F32)
    tile = block[PART:BLOCK].astype(F32)
    lse = []
    for e in range(2):
        mine = lane_of(place, e)
        for t in range(STEPS):
            x = tile[t : t + 1] + tile[2 + t : 3 + t] + tile[4 + t : 5 + t]
            spread = jnp.where(mine, jnp.broadcast_to(x, (GROUP, 128)), 0.0)
            lse.append(jnp.sum(spread, axis=1, keepdims=True))
    return o, jnp.concatenate(lse, axis=0)


def merge(state, parts):
    top = parts[0][1] if state is None else state[0]
    for _, lse in parts:
        top = jnp.maximum(top, lse)
    total, weighted = None, None
    if state is not None:
        factor = jnp.exp2(state[0] - top)
        total, weighted = state[1] * factor, state[2] * factor
    for o, lse in parts:
        factor = jnp.exp2(lse - top)
        total = factor if total is None else total + factor
        weighted = o * factor if weighted is None else weighted + o * factor
    return top, total, weighted


def order(me, plane):
    across, high = me // 2, me % 2
    units = [
        ((across + dx) % 4) * 2 + (high + dy) % 2
        for dx, dy in ((0, 0), (0, 1), (1, 0), (3, 0), (1, 1), (3, 1), (2, 0), (2, 1))
    ]

    def is_far(u):
        f = (u - plane + UNITS) % UNITS
        return (f >= 2) & (f <= 6)

    def rank(u):
        f = (u - plane + UNITS) % UNITS
        return jnp.where(f == 7, 0, jnp.where(f == 1, 1, 2))

    one = jnp.int32(1)
    count = one
    for u in units[1:]:
        count = count + jnp.where(is_far(u), 1, 0)
    own_rank = jnp.where(is_far(me), 3, rank(me))
    held_back = (plane + 2) % UNITS
    places, n = [jnp.int32(0)], one
    for u in units[1:]:
        near_place = count + rank(u) - jnp.where(own_rank < rank(u), 1, 0)
        late = (u == held_back) & jnp.logical_not(is_far(me))
        places.append(jnp.where(late, count - 1, jnp.where(is_far(u), n, near_place)))
        n = n + jnp.where(is_far(u) & jnp.logical_not(late), 1, 0)

    def unit_at(i):
        return sum(jnp.where(at == i, u, 0) for u, at in zip(units, places))

    def position(v):
        return sum(jnp.where(u == v, at, 0) for u, at in zip(units, places))

    return units, position, unit_at, is_far


def attend(
    lengths_hbm, q_hbm, kv_hbm, out_ref,
    lengths, kv, qs, hide, s0, s1, spill, psend, precv, zsend, recv,
    kv_sem, own_sem, len_sem, q_out, q_in, p_out, p_in, m_out, m_in, z_out,
):
    scores = (s0, s1)
    me = lax.axis_index("kv")
    ctx = lax.axis_index("ctx")
    plane = ctx // 4
    place = ctx % 4
    flip = 2 - 4 * (place // 2)
    units, position, unit_at, is_far = order(me, plane)

    def kv_copy(p):
        return pltpu.make_async_copy(kv_hbm.at[0, p], kv.at[p], kv_sem.at[p])

    def peer(k):
        return (k, ctx + ((k + me) % 2) * flip)

    def query_copy(k, source):
        return pltpu.make_async_remote_copy(
            src_ref=q_hbm.at[:, pl.ds(pl.multiple_of(k * WIDE, WIDE), WIDE)],
            dst_ref=qs.at[source],
            send_sem=q_out.at[k],
            recv_sem=q_in.at[source],
            device_id=peer(k),
            device_id_type=MESH,
        )

    def part_copy(i, u, d):
        return pltpu.make_async_remote_copy(
            src_ref=psend.at[i, d],
            dst_ref=recv.at[ctx],
            send_sem=p_out.at[i, d],
            recv_sem=p_in.at[ctx],
            device_id=(me, u * 4 + d),
            device_id_type=MESH,
        )

    def arrival(source):
        return pltpu.make_async_remote_copy(
            src_ref=psend.at[0, 0],
            dst_ref=recv.at[source],
            send_sem=p_out.at[0, 0],
            recv_sem=p_in.at[source],
            device_id=(me, source),
            device_id_type=MESH,
        )

    def mate_copy(i, o):
        there = (place + o) % 4
        return pltpu.make_async_remote_copy(
            src_ref=psend.at[i, there],
            dst_ref=precv.at[i, o - 1],
            send_sem=m_out.at[i, o - 1],
            recv_sem=m_in.at[i, o - 1],
            device_id=(me, plane * 4 + there),
            device_id_type=MESH,
        )

    def far_copy(i, u):
        return pltpu.make_async_remote_copy(
            src_ref=zsend.at[i],
            dst_ref=recv.at[ctx],
            send_sem=z_out.at[i],
            recv_sem=p_in.at[ctx],
            device_id=(me, u * 4 + place),
            device_id_type=MESH,
        )

    def fresh(i, u):
        return position(u + 1 - 2 * (u % 2)) > i

    measures = pltpu.make_async_copy(lengths_hbm, lengths, len_sem)
    measures.start()
    own = pltpu.make_async_copy(
        q_hbm.at[:, pl.ds(pl.multiple_of(me * WIDE, WIDE), WIDE)], qs.at[me], own_sem
    )
    own.start()

    def fetch(i, _):
        u = unit_at(i)

        @pl.when(fresh(i, u))
        def _():
            kv_copy(u // 2).start()

        return 0

    lax.fori_loop(0, UNITS, fetch, 0)

    barrier = pltpu.get_barrier_semaphore()
    for n in range(1, UNITS):
        pl.semaphore_signal(
            barrier, inc=1, device_id=peer((me + n) % UNITS), device_id_type=MESH
        )
    greeted = UNITS - 1
    for f in range(UNITS):
        for d in range(4):
            there = ((plane + f) % UNITS) * 4
            if f == 0 and d:
                there = there + (place + d) % 4
            elif f in (1, 7):
                there = there + d
            elif f and not d:
                there = there + place
            else:
                continue
            greeted += 1
            pl.semaphore_signal(barrier, inc=1, device_id=(me, there), device_id_type=MESH)
    pl.semaphore_wait(barrier, greeted)

    def send_queries(low, high):
        for u in units[low : high + 1]:
            query_copy(u, me).start()

    send_queries(1, 3)
    measures.wait()
    limits = limit_lanes(lengths) - ctx * SPAN

    def fill(i, _):
        at_row = lax.broadcasted_iota(jnp.int32, (64, 128), 0) + i * 64
        at = pl.ds(pl.multiple_of(i * 64, 64), 64)
        hide[at, :] = jnp.where(at_row < limits[0:1, :], 0.0, -HIDE).astype(BF16)
        return 0

    lax.fori_loop(0, SPAN // 64, fill, 0)
    own.wait()

    def ready(i, u):
        @pl.when(u != me)
        def _():
            query_copy(u, u).wait_recv()

        @pl.when(fresh(i, u))
        def _():
            kv_copy(u // 2).wait()

    def marked(u):
        wide = qs[u].astype(F32)
        q = jnp.concatenate(
            [
                wide[t * 8 : t * 8 + 8, h * HEAD : (h + 1) * HEAD]
                for t in range(STEPS)
                for h in range(GROUP)
            ],
            axis=0,
        ).astype(BF16)
        i = lax.broadcasted_iota(jnp.int32, (UNIT_ROWS, 128), 0)
        lane = lax.broadcasted_iota(jnp.int32, (UNIT_ROWS, 128), 1)
        target = (i // 128) * ROWS + u * 8 + i % 8
        return jnp.concatenate([q, (lane == target).astype(BF16)], axis=1)

    ones = jnp.ones((CHUNK, 128), BF16)

    def stage(i, u, n, use, make, top):
        if u is not None:
            peak = jnp.max(top, axis=1, keepdims=True) * SCALE
            total = None
        if n is not None:
            q = marked(n)
            new_top = None
        for c in range(SPAN // CHUNK):
            at = slice(c * CHUNK, (c + 1) * CHUNK)
            if n is not None:
                k = jnp.concatenate([kv[n // 2, at, 0:HEAD], hide[at, :]], axis=1)
                s = nt(q, k)
                scores[make][:, at] = s
                for b in range(CHUNK // 128):
                    x = s[:, b * 128 : (b + 1) * 128]
                    new_top = x if new_top is None else jnp.maximum(new_top, x)
            if u is not None:
                w = jnp.exp2(scores[use][:, at] * SCALE - peak).astype(BF16)
                v = jnp.concatenate([kv[u // 2, at, HEAD : 2 * HEAD], ones], axis=1)
                part = jnp.dot(w, v, preferred_element_type=F32)
                total = part if total is None else total + part
        if u is not None:
            weight = total[:, HEAD:]
            lse = jnp.log2(weight) + peak
            sums = pack((lse[:128], lse[128:]))
            spill[...] = total[:, :HEAD] / weight
            for d in range(4):
                for e in range(2):
                    rows = spill[pl.ds(2 * d + e, 32, stride=8), :]
                    psend[i, d, e * 32 : e * 32 + 32, :] = rows.astype(BF16)
                psend[i, d, PART:BLOCK, :] = sums
        return new_top if n is not None else None

    def send_near(i, u):
        for d in range(4):

            @pl.when(u * 4 + d != ctx)
            def _():
                part_copy(i, u, d).start()

    def send(i, u):
        @pl.when(is_far(u))
        def _():
            for o in range(1, 4):
                mate_copy(i, o).start()

        @pl.when(jnp.logical_not(is_far(u)))
        def _():
            send_near(i, u)

    def pass_on(i, u):
        @pl.when(is_far(u))
        def _():
            for o in range(1, 4):
                mate_copy(i, o).wait_recv()
            parts = [unpack(psend[i, place], place)]
            for o in range(1, 4):
                parts.append(unpack(precv[i, o - 1], place))
            top, total, weighted = merge(None, parts)
            zsend[i, 0:PART, :] = (weighted / total).astype(BF16)
            zsend[i, PART:BLOCK, :] = pack_part(jnp.log2(total) + top, place)
            far_copy(i, u).start()

    ready(0, me)
    top = stage(0, None, me, 1, 0, None)
    send_queries(4, 5)
    stage(0, me, None, 0, None, top)
    send(0, me)
    second = unit_at(1)
    send_queries(6, 7)
    ready(1, second)
    top = stage(1, None, second, None, 1, None)

    def pair(h, top):
        i = 2 * h + 1
        a, b, c = unit_at(i), unit_at(i + 1), unit_at(i + 2)
        ready(i + 1, b)
        top = stage(i, a, b, 1, 0, top)
        send(i, a)

        @pl.when(h > 0)
        def _():
            pass_on(i - 2, unit_at(i - 2))

        ready(i + 2, c)
        top = stage(i + 1, b, c, 0, 1, top)
        send(i + 1, b)
        pass_on(i - 1, unit_at(i - 1))
        return top

    top = lax.fori_loop(0, 3, pair, top)
    final = unit_at(UNITS - 1)
    stage(UNITS - 1, final, None, 1, None, top)
    send_near(UNITS - 1, final)
    pass_on(UNITS - 3, unit_at(UNITS - 3))

    mine = psend[position(plane), place]
    state = merge(None, [unpack(mine, place)])

    def take(state, sources):
        for source in sources:
            arrival(source).wait_recv()
        return merge(state, [unpack(recv[source], place) for source in sources])

    state = take(state, [((plane + f) % UNITS) * 4 + place for f in range(2, 7)])
    for f in (7, 1):
        state = take(state, [((plane + f) % UNITS) * 4 + d for d in range(4)])
    parts = []
    for o in range(1, 4):
        source = plane * 4 + (place + o) % 4
        arrival(source).wait_recv()
        parts.append(unpack(recv[source], place))
    _, total, weighted = merge(state, parts)
    out = weighted / total
    for t in range(STEPS):
        for h in range(GROUP):
            k = t * GROUP + h
            both = jnp.concatenate([out[k : k + 1], out[32 + k : 33 + k]], axis=0)
            out_ref[t, :, h * HEAD : (h + 1) * HEAD] = both.astype(BF16)

    for n in range(1, UNITS):
        query_copy((me + n) % UNITS, me).wait_send()

    def sent(i, _):
        u = unit_at(i)

        @pl.when(is_far(u))
        def _():
            for o in range(1, 4):
                mate_copy(i, o).wait_send()
            far_copy(i, u).wait_send()

        @pl.when(jnp.logical_not(is_far(u)))
        def _():
            for d in range(4):

                @pl.when(u * 4 + d != ctx)
                def _():
                    part_copy(i, u, d).wait_send()

        return 0

    lax.fori_loop(0, UNITS, sent, 0)


def shards(queries, kv_cache, lengths):
    out = pl.pallas_call(
        attend,
        out_shape=jax.ShapeDtypeStruct((STEPS, 2, WIDE), BF16),
        in_specs=[pl.BlockSpec(memory_space=pltpu.HBM)] * 3,
        out_specs=pl.BlockSpec(memory_space=pltpu.VMEM),
        scratch_shapes=[
            pltpu.SMEM((ROWS,), jnp.int32),
            pltpu.VMEM((PROMPTS, SPAN, 2 * HEAD), BF16),
            pltpu.VMEM((UNITS, STEPS * 8, WIDE), BF16),
            pltpu.VMEM((SPAN, 128), BF16),
            pltpu.VMEM((UNIT_ROWS, SPAN), F32),
            pltpu.VMEM((UNIT_ROWS, SPAN), F32),
            pltpu.VMEM((UNIT_ROWS, HEAD), F32),
            pltpu.VMEM((UNITS, 4, BLOCK, HEAD), BF16),
            pltpu.VMEM((UNITS, 3, BLOCK, HEAD), BF16),
            pltpu.VMEM((UNITS, BLOCK, HEAD), BF16),
            pltpu.VMEM((32, BLOCK, HEAD), BF16),
            pltpu.SemaphoreType.DMA((PROMPTS,)),
            pltpu.SemaphoreType.DMA,
            pltpu.SemaphoreType.DMA,
            pltpu.SemaphoreType.DMA((UNITS,)),
            pltpu.SemaphoreType.DMA((UNITS,)),
            pltpu.SemaphoreType.DMA((UNITS, 4)),
            pltpu.SemaphoreType.DMA((32,)),
            pltpu.SemaphoreType.DMA((UNITS, 3)),
            pltpu.SemaphoreType.DMA((UNITS, 3)),
            pltpu.SemaphoreType.DMA((UNITS,)),
        ],
        compiler_params=pltpu.CompilerParams(
            vmem_limit_bytes=60 * 2**20, collective_id=0, has_side_effects=True
        ),
        name="attend",
    )(lengths, queries.reshape(STEPS * 8, UNITS * WIDE), kv_cache)
    return out


def solution(mesh):
    in_specs = (P(None, "kv", None), P("kv", None, "ctx", None), P())
    out_specs = P(None, "ctx", "kv")
    return jax.shard_map(shards, mesh=mesh, in_specs=in_specs, out_specs=out_specs, check_vma=False)
```

time: 41 us -> 36.3 us (0.89)
  the two profiles are of different devices: /device:TPU:24 before, /device:TPU:12 now
where the time goes in v3:
time: 36.3 us; the launch traced here: 36.1 us
  Pallas kernels  34.8 us (96%)
  local copies, waits for them, and re-layouts  1.34 us (4%)
    pallas_call x1, Pallas kernels, shards(): pl.pallas_call(attend, out_shape=jax.ShapeDtypeStruct((STEPS, 2, WIDE), B...  34.8 us
    unnamed x1, local copies, waits for them, and re-layouts  1.34 us

profile of v3, /device:TPU:12, one launch (start us, length us, event | category | flops | bytes accessed | tf_op | source)
XLA Modules:
  0.0 36.1 jit_solution(5302968652666261624)
XLA Ops:
  0.0 34.8 %attend.1 = bf16[2,2,2048]{2,1,0:T(2,128)(2,1)} custom-call(s32[64]{0:T(128)} %lengths_hbm.1, bf16[16,16384]{1,0:T(8,128)(2,1)} %bitcast.1, bf16[1,4,4096,256]{3,2,1,0:T(8,128)(2,1)} %kv_hbm.1), custom_call_target="tpu_custom_call" | custom-call | tf_op jit(solution)/shard_map/attend/pallas_call | solution.py:438
  34.8 1.3 %copy.5 = bf16[2,2,2048]{2,1,0:T(2,128)(2,1)} copy(bf16[2,2,2048]{2,1,0:T(2,128)(2,1)} %attend.1) | data formatting | bytes 32768

commit v4 on v3

--- a/solution.py
+++ b/solution.py
@@ -108,22 +108,24 @@
         f = (u - plane + UNITS) % UNITS
         return (f >= 2) & (f <= 6)
 
+    lower = jnp.minimum((plane + 1) % UNITS, (plane + 7) % UNITS)
+
     def rank(u):
-        f = (u - plane + UNITS) % UNITS
-        return jnp.where(f == 7, 0, jnp.where(f == 1, 1, 2))
+        return jnp.where(u == plane, 2, jnp.where(u == lower, 0, 1))
 
     one = jnp.int32(1)
     count = one
     for u in units[1:]:
         count = count + jnp.where(is_far(u), 1, 0)
     own_rank = jnp.where(is_far(me), 3, rank(me))
-    held_back = (plane + 2) % UNITS
+    last_far = jnp.maximum((plane + 2) % UNITS, (plane + 6) % UNITS)
+    other = jnp.maximum((plane + 3) % UNITS, (plane + 5) % UNITS)
+    last_far = jnp.where(last_far == me, other, last_far)
     places, n = [jnp.int32(0)], one
     for u in units[1:]:
         near_place = count + rank(u) - jnp.where(own_rank < rank(u), 1, 0)
-        late = (u == held_back) & jnp.logical_not(is_far(me))
-        places.append(jnp.where(late, count - 1, jnp.where(is_far(u), n, near_place)))
-        n = n + jnp.where(is_far(u) & jnp.logical_not(late), 1, 0)
+        places.append(jnp.where(u == last_far, count - 1, jnp.where(is_far(u), n, near_place)))
+        n = n + jnp.where(is_far(u) & (u != last_far), 1, 0)
 
     def unit_at(i):
         return sum(jnp.where(at == i, u, 0) for u, at in zip(units, places))
@@ -137,7 +139,7 @@
 def attend(
     lengths_hbm, q_hbm, kv_hbm, out_ref,
     lengths, kv, qs, hide, s0, s1, spill, psend, precv, zsend, recv,
-    kv_sem, own_sem, len_sem, q_out, q_in, p_out, p_in, m_out, m_in, z_out,
+    kv_sem, own_sem, len_sem, q_out, q_in, b_out, b_in, m_in,
 ):
     scores = (s0, s1)
     me = lax.axis_index("kv")
@@ -157,7 +159,7 @@
         return pltpu.make_async_remote_copy(
             src_ref=q_hbm.at[:, pl.ds(pl.multiple_of(k * WIDE, WIDE), WIDE)],
             dst_ref=qs.at[source],
-            send_sem=q_out.at[k],
+            send_sem=q_out,
             recv_sem=q_in.at[source],
             device_id=peer(k),
             device_id_type=MESH,
@@ -167,19 +169,19 @@
         return pltpu.make_async_remote_copy(
             src_ref=psend.at[i, d],
             dst_ref=recv.at[ctx],
-            send_sem=p_out.at[i, d],
-            recv_sem=p_in.at[ctx],
+            send_sem=b_out,
+            recv_sem=b_in.at[jnp.where(u == plane, 2, 1)],
             device_id=(me, u * 4 + d),
             device_id_type=MESH,
         )
 
-    def arrival(source):
+    def blocks(ref, count, sem):
         return pltpu.make_async_remote_copy(
-            src_ref=psend.at[0, 0],
-            dst_ref=recv.at[source],
-            send_sem=p_out.at[0, 0],
-            recv_sem=p_in.at[source],
-            device_id=(me, source),
+            src_ref=ref.at[pl.ds(0, count)],
+            dst_ref=ref.at[pl.ds(0, count)],
+            send_sem=sem,
+            recv_sem=sem,
+            device_id=(me, ctx),
             device_id_type=MESH,
         )
 
@@ -188,8 +190,8 @@
         return pltpu.make_async_remote_copy(
             src_ref=psend.at[i, there],
             dst_ref=precv.at[i, o - 1],
-            send_sem=m_out.at[i, o - 1],
-            recv_sem=m_in.at[i, o - 1],
+            send_sem=b_out,
+            recv_sem=m_in.at[i],
             device_id=(me, plane * 4 + there),
             device_id_type=MESH,
         )
@@ -198,8 +200,8 @@
         return pltpu.make_async_remote_copy(
             src_ref=zsend.at[i],
             dst_ref=recv.at[ctx],
-            send_sem=z_out.at[i],
-            recv_sem=p_in.at[ctx],
+            send_sem=b_out,
+            recv_sem=b_in.at[0],
             device_id=(me, u * 4 + place),
             device_id_type=MESH,
         )
@@ -261,6 +263,7 @@
         return 0
 
     lax.fori_loop(0, SPAN // 64, fill, 0)
+    send_queries(4, 5)
     own.wait()
 
     def ready(i, u):
@@ -322,86 +325,82 @@
                 psend[i, d, PART:BLOCK, :] = sums
         return new_top if n is not None else None
 
+    def send_mates(i):
+        for o in range(1, 4):
+            mate_copy(i, o).start()
+
     def send_near(i, u):
-        for d in range(4):
-
-            @pl.when(u * 4 + d != ctx)
-            def _():
-                part_copy(i, u, d).start()
+        for o in range(1, 4):
+            part_copy(i, u, (place + o) % 4).start()
+
+        @pl.when(u != plane)
+        def _():
+            part_copy(i, u, place).start()
 
     def send(i, u):
         @pl.when(is_far(u))
         def _():
-            for o in range(1, 4):
-                mate_copy(i, o).start()
+            send_mates(i)
 
         @pl.when(jnp.logical_not(is_far(u)))
         def _():
             send_near(i, u)
 
     def pass_on(i, u):
-        @pl.when(is_far(u))
-        def _():
-            for o in range(1, 4):
-                mate_copy(i, o).wait_recv()
-            parts = [unpack(psend[i, place], place)]
-            for o in range(1, 4):
-                parts.append(unpack(precv[i, o - 1], place))
-            top, total, weighted = merge(None, parts)
-            zsend[i, 0:PART, :] = (weighted / total).astype(BF16)
-            zsend[i, PART:BLOCK, :] = pack_part(jnp.log2(total) + top, place)
-            far_copy(i, u).start()
-
+        blocks(recv, 3, m_in.at[i]).wait_recv()
+        parts = [unpack(psend[i, place], place)]
+        for o in range(1, 4):
+            parts.append(unpack(precv[i, o - 1], place))
+        top, total, weighted = merge(None, parts)
+        zsend[i, 0:PART, :] = (weighted / total).astype(BF16)
+        zsend[i, PART:BLOCK, :] = pack_part(jnp.log2(total) + top, place)
+        far_copy(i, u).start()
+
+    at = [unit_at(i) for i in range(UNITS)]
     ready(0, me)
     top = stage(0, None, me, 1, 0, None)
-    send_queries(4, 5)
+    send_queries(6, 7)
     stage(0, me, None, 0, None, top)
     send(0, me)
-    second = unit_at(1)
-    send_queries(6, 7)
-    ready(1, second)
-    top = stage(1, None, second, None, 1, None)
-
-    def pair(h, top):
-        i = 2 * h + 1
-        a, b, c = unit_at(i), unit_at(i + 1), unit_at(i + 2)
-        ready(i + 1, b)
-        top = stage(i, a, b, 1, 0, top)
-        send(i, a)
-
-        @pl.when(h > 0)
-        def _():
-            pass_on(i - 2, unit_at(i - 2))
-
-        ready(i + 2, c)
-        top = stage(i + 1, b, c, 0, 1, top)
-        send(i + 1, b)
-        pass_on(i - 1, unit_at(i - 1))
-        return top
-
-    top = lax.fori_loop(0, 3, pair, top)
-    final = unit_at(UNITS - 1)
-    stage(UNITS - 1, final, None, 1, None, top)
-    send_near(UNITS - 1, final)
-    pass_on(UNITS - 3, unit_at(UNITS - 3))
+    ready(1, at[1])
+    top = stage(1, None, at[1], None, 1, None)
+    for i in range(1, UNITS - 1):
+        ready(i + 1, at[i + 1])
+        top = stage(i, at[i], at[i + 1], i % 2, (i + 1) % 2, top)
+        if i <= 4:
+            send_mates(i)
+        elif i == 5:
+            send(i, at[i])
+        else:
+            send_near(i, at[i])
+        if i == 3:
+
+            @pl.when(is_far(me))
+            def _():
+                pass_on(0, me)
+
+        elif i > 3:
+            pass_on(i - 3, at[i - 3])
+    stage(UNITS - 1, at[UNITS - 1], None, 1, None, top)
+    send_near(UNITS - 1, at[UNITS - 1])
+
+    pass_on(4, at[4])
+
+    @pl.when(is_far(at[5]))
+    def _():
+        pass_on(5, at[5])
 
     mine = psend[position(plane), place]
     state = merge(None, [unpack(mine, place)])
 
-    def take(state, sources):
-        for source in sources:
-            arrival(source).wait_recv()
+    def take(state, sources, kind):
+        blocks(recv, len(sources), b_in.at[kind]).wait_recv()
         return merge(state, [unpack(recv[source], place) for source in sources])
 
-    state = take(state, [((plane + f) % UNITS) * 4 + place for f in range(2, 7)])
-    for f in (7, 1):
-        state = take(state, [((plane + f) % UNITS) * 4 + d for d in range(4)])
-    parts = []
-    for o in range(1, 4):
-        source = plane * 4 + (place + o) % 4
-        arrival(source).wait_recv()
-        parts.append(unpack(recv[source], place))
-    _, total, weighted = merge(state, parts)
+    state = take(state, [((plane + f) % UNITS) * 4 + place for f in range(2, 7)], 0)
+    state = take(state, [plane * 4 + (place + o) % 4 for o in range(1, 4)], 2)
+    sources = [((plane + f) % UNITS) * 4 + d for f in (1, 7) for d in range(4)]
+    _, total, weighted = take(state, sources, 1)
     out = weighted / total
     for t in range(STEPS):
         for h in range(GROUP):
@@ -409,29 +408,15 @@
             both = jnp.concatenate([out[k : k + 1], out[32 + k : 33 + k]], axis=0)
             out_ref[t, :, h * HEAD : (h + 1) * HEAD] = both.astype(BF16)
 
-    for n in range(1, UNITS):
-        query_copy((me + n) % UNITS, me).wait_send()
-
-    def sent(i, _):
-        u = unit_at(i)
-
-        @pl.when(is_far(u))
-        def _():
-            for o in range(1, 4):
-                mate_copy(i, o).wait_send()
-            far_copy(i, u).wait_send()
-
-        @pl.when(jnp.logical_not(is_far(u)))
-        def _():
-            for d in range(4):
-
-                @pl.when(u * 4 + d != ctx)
-                def _():
-                    part_copy(i, u, d).wait_send()
-
-        return 0
-
-    lax.fori_loop(0, UNITS, sent, 0)
+    pltpu.make_async_remote_copy(
+        src_ref=qs.at[pl.ds(0, UNITS - 1)],
+        dst_ref=qs.at[pl.ds(0, UNITS - 1)],
+        send_sem=q_out,
+        recv_sem=q_out,
+        device_id=(me, ctx),
+        device_id_type=MESH,
+    ).wait_send()
+    blocks(recv, 5 * 4 + 2 * 4 + 3, b_out).wait_send()
 
 
 def shards(queries, kv_cache, lengths):
@@ -455,12 +440,10 @@
             pltpu.SemaphoreType.DMA((PROMPTS,)),
             pltpu.SemaphoreType.DMA,
             pltpu.SemaphoreType.DMA,
+            pltpu.SemaphoreType.DMA,
             pltpu.SemaphoreType.DMA((UNITS,)),
-            pltpu.SemaphoreType.DMA((UNITS,)),
-            pltpu.SemaphoreType.DMA((UNITS, 4)),
-            pltpu.SemaphoreType.DMA((32,)),
-            pltpu.SemaphoreType.DMA((UNITS, 3)),
-            pltpu.SemaphoreType.DMA((UNITS, 3)),
+            pltpu.SemaphoreType.DMA,
+            pltpu.SemaphoreType.DMA((3,)),
             pltpu.SemaphoreType.DMA((UNITS,)),
         ],
         compiler_params=pltpu.CompilerParams(

time: 36.3 us -> 33.8 us (0.931)
  Pallas kernels: 34.8 us -> 32 us
    pallas_call x1, Pallas kernels: 34.8 us -> 32 us  [shards(): pl.pallas_call(attend, out_shape=jax.ShapeDtypeStruct((STEPS, 2, WIDE), B...]
where the time goes in v4:
time: 33.8 us; the launch traced here: 33.4 us
  Pallas kernels  32 us (95%)
  local copies, waits for them, and re-layouts  1.34 us (4%)
    pallas_call x1, Pallas kernels, shards(): pl.pallas_call(attend, out_shape=jax.ShapeDtypeStruct((STEPS, 2, WIDE), B...  32 us
    unnamed x1, local copies, waits for them, and re-layouts  1.34 us

profile of v4, /device:TPU:12, one launch (start us, length us, event | category | flops | bytes accessed | tf_op | source)
XLA Modules:
  0.0 33.4 jit_solution(1869171509830957747)
XLA Ops:
  0.0 32.0 %attend.1 = bf16[2,2,2048]{2,1,0:T(2,128)(2,1)} custom-call(s32[64]{0:T(128)} %lengths_hbm.1, bf16[16,16384]{1,0:T(8,128)(2,1)} %bitcast.1, bf16[1,4,4096,256]{3,2,1,0:T(8,128)(2,1)} %kv_hbm.1), custom_call_target="tpu_custom_call" | custom-call | tf_op jit(solution)/shard_map/attend/pallas_call | solution.py:423
  32.0 1.3 %copy.5 = bf16[2,2,2048]{2,1,0:T(2,128)(2,1)} copy(bf16[2,2,2048]{2,1,0:T(2,128)(2,1)} %attend.1) | data formatting | bytes 32768

commit v5 on v4

--- a/solution.py
+++ b/solution.py
@@ -14,7 +14,7 @@
 BLOCK = PART + 16
 SCALE = 1.4426950408889634 / HEAD**0.5
 HIDE = 2.0**20
-CHUNK = 1024
+CHUNK = 512
 MESH = pl.DeviceIdType.MESH
 
 
@@ -111,7 +111,8 @@
     lower = jnp.minimum((plane + 1) % UNITS, (plane + 7) % UNITS)
 
     def rank(u):
-        return jnp.where(u == plane, 2, jnp.where(u == lower, 0, 1))
+        early = jnp.where(plane < 4, 1, 0)
+        return jnp.where(u == plane, 2 - early, jnp.where(u == lower, 0, 1 + early))
 
     one = jnp.int32(1)
     count = one
@@ -147,7 +148,6 @@
     plane = ctx // 4
     place = ctx % 4
     flip = 2 - 4 * (place // 2)
-    units, position, unit_at, is_far = order(me, plane)
 
     def kv_copy(p):
         return pltpu.make_async_copy(kv_hbm.at[0, p], kv.at[p], kv_sem.at[p])
@@ -170,7 +170,7 @@
             src_ref=psend.at[i, d],
             dst_ref=recv.at[ctx],
             send_sem=b_out,
-            recv_sem=b_in.at[jnp.where(u == plane, 2, 1)],
+            recv_sem=b_in.at[jnp.where(u == plane, 2, jnp.where(u == (plane + 1) % UNITS, 3, 1))],
             device_id=(me, u * 4 + d),
             device_id_type=MESH,
         )
@@ -206,27 +206,7 @@
             device_id_type=MESH,
         )
 
-    def fresh(i, u):
-        return position(u + 1 - 2 * (u % 2)) > i
-
-    measures = pltpu.make_async_copy(lengths_hbm, lengths, len_sem)
-    measures.start()
-    own = pltpu.make_async_copy(
-        q_hbm.at[:, pl.ds(pl.multiple_of(me * WIDE, WIDE), WIDE)], qs.at[me], own_sem
-    )
-    own.start()
-
-    def fetch(i, _):
-        u = unit_at(i)
-
-        @pl.when(fresh(i, u))
-        def _():
-            kv_copy(u // 2).start()
-
-        return 0
-
-    lax.fori_loop(0, UNITS, fetch, 0)
-
+    kv_copy(me // 2).start()
     barrier = pltpu.get_barrier_semaphore()
     for n in range(1, UNITS):
         pl.semaphore_signal(
@@ -246,6 +226,16 @@
                 continue
             greeted += 1
             pl.semaphore_signal(barrier, inc=1, device_id=(me, there), device_id_type=MESH)
+    units, position, unit_at, is_far = order(me, plane)
+    measures = pltpu.make_async_copy(lengths_hbm, lengths, len_sem)
+    measures.start()
+    own = pltpu.make_async_copy(
+        q_hbm.at[:, pl.ds(pl.multiple_of(me * WIDE, WIDE), WIDE)], qs.at[me], own_sem
+    )
+    own.start()
+    others = [(me // 2 + n) % PROMPTS for n in range(1, PROMPTS)]
+    for p in others:
+        kv_copy(p).start()
     pl.semaphore_wait(barrier, greeted)
 
     def send_queries(low, high):
@@ -265,15 +255,6 @@
     lax.fori_loop(0, SPAN // 64, fill, 0)
     send_queries(4, 5)
     own.wait()
-
-    def ready(i, u):
-        @pl.when(u != me)
-        def _():
-            query_copy(u, u).wait_recv()
-
-        @pl.when(fresh(i, u))
-        def _():
-            kv_copy(u // 2).wait()
 
     def marked(u):
         wide = qs[u].astype(F32)
@@ -357,15 +338,17 @@
         far_copy(i, u).start()
 
     at = [unit_at(i) for i in range(UNITS)]
-    ready(0, me)
+    kv_copy(me // 2).wait()
     top = stage(0, None, me, 1, 0, None)
     send_queries(6, 7)
     stage(0, me, None, 0, None, top)
     send(0, me)
-    ready(1, at[1])
+    for p in others:
+        kv_copy(p).wait()
+    query_copy(at[1], at[1]).wait_recv()
     top = stage(1, None, at[1], None, 1, None)
     for i in range(1, UNITS - 1):
-        ready(i + 1, at[i + 1])
+        query_copy(at[i + 1], at[i + 1]).wait_recv()
         top = stage(i, at[i], at[i + 1], i % 2, (i + 1) % 2, top)
         if i <= 4:
             send_mates(i)
@@ -399,8 +382,8 @@
 
     state = take(state, [((plane + f) % UNITS) * 4 + place for f in range(2, 7)], 0)
     state = take(state, [plane * 4 + (place + o) % 4 for o in range(1, 4)], 2)
-    sources = [((plane + f) % UNITS) * 4 + d for f in (1, 7) for d in range(4)]
-    _, total, weighted = take(state, sources, 1)
+    state = take(state, [((plane + 1) % UNITS) * 4 + d for d in range(4)], 1)
+    _, total, weighted = take(state, [((plane + 7) % UNITS) * 4 + d for d in range(4)], 3)
     out = weighted / total
     for t in range(STEPS):
         for h in range(GROUP):
@@ -443,7 +426,7 @@
             pltpu.SemaphoreType.DMA,
             pltpu.SemaphoreType.DMA((UNITS,)),
             pltpu.SemaphoreType.DMA,
-            pltpu.SemaphoreType.DMA((3,)),
+            pltpu.SemaphoreType.DMA((4,)),
             pltpu.SemaphoreType.DMA((UNITS,)),
         ],
         compiler_params=pltpu.CompilerParams(

time: 33.8 us -> 33.5 us (level)
  Pallas kernels: 32 us -> 31.6 us
    pallas_call x1, Pallas kernels: 32 us -> 31.6 us  [shards(): pl.pallas_call(attend, out_shape=jax.ShapeDtypeStruct((STEPS, 2, WIDE), B...]
where the time goes in v5:
time: 33.5 us; the launch traced here: 32.9 us
  Pallas kernels  31.6 us (94%)
  local copies, waits for them, and re-layouts  1.34 us (4%)
    pallas_call x1, Pallas kernels, shards(): pl.pallas_call(attend, out_shape=jax.ShapeDtypeStruct((STEPS, 2, WIDE), B...  31.6 us
    unnamed x1, local copies, waits for them, and re-layouts  1.34 us

profile of v5, /device:TPU:12, one launch (start us, length us, event | category | flops | bytes accessed | tf_op | source)
XLA Modules:
  0.0 32.9 jit_solution(18251662429172644762)
XLA Ops:
  0.0 31.6 %attend.1 = bf16[2,2,2048]{2,1,0:T(2,128)(2,1)} custom-call(s32[64]{0:T(128)} %lengths_hbm.1, bf16[16,16384]{1,0:T(8,128)(2,1)} %bitcast.1, bf16[1,4,4096,256]{3,2,1,0:T(8,128)(2,1)} %kv_hbm.1), custom_call_target="tpu_custom_call" | custom-call | tf_op jit(solution)/shard_map/attend/pallas_call | solution.py:406
  31.6 1.3 %copy.5 = bf16[2,2,2048]{2,1,0:T(2,128)(2,1)} copy(bf16[2,2,2048]{2,1,0:T(2,128)(2,1)} %attend.1) | data formatting | bytes 32768
